TPU v7x, 128 devices: a whole 4x4x4 slice. The times are simulated.
128 devices in a mesh: dp: 16 (over z, x_hi, core), pipe: 8 (over x_lo, y).
Axes of the slice: x: 4 (x_hi: 2, x_lo: 2; x = x_hi * 2 + x_lo), y: 4, z: 4, core: 2. Of those that a mesh axis runs over, the one named last changes fastest.
Arguments:
- inputs: bfloat16 [4, 1024, 8192], P(None, 'dp'), may hold values from -6 to 6
- targets: int32 [4, 1024], P(None, 'dp'), may hold values from 0 to 511
- adapter_down: bfloat16 [8, 8192, 256], P('pipe'), may hold values from -0.0625 to 0.0625
- adapter_up: bfloat16 [8, 256, 8192], P('pipe'), may hold values from -0.375 to 0.375
- value_weight: float32 [8192], replicated, may hold values from -0.0625 to 0.0625
- returns: float32 [512], replicated, may hold values from -6 to 6
Outputs:
- grad_down: float32 [8, 8192, 256], P('pipe', 'dp')
- grad_up: float32 [8, 256, 8192], P('pipe', None, 'dp')
All inputs are finite; a program needn't handle non-finite values.
Results may differ from a plain program's by a relative error of at most 0.024.
Values may be sent and summed in bfloat16 or wider, within the bound.
A program may use at most 128 MiB of HBM per device.

v0:
```python
import jax
import jax.numpy as jnp
from jax import lax
from jax.sharding import PartitionSpec as P


def from_behind(value, axis, steps):
    count = lax.axis_size(axis)
    first, last = (max(0, -steps), min(count, count - steps))
    return lax.ppermute(value, axis, [(source, source + steps) for source in range(first, last)])


def norm_rows(values):
    floats = values.astype(jnp.float32)
    factor = lax.rsqrt(jnp.mean(floats * floats, axis=-1, keepdims=True) + 1e-05)
    return (floats * factor, factor)


def contract_last(left, right):
    return lax.dot_general(
        left, right, (((1,), (1,)), ((), ())), preferred_element_type=jnp.float32
    )


def contract_rows(left, right):
    return lax.dot_general(
        left, right, (((0,), (0,)), ((), ())), preferred_element_type=jnp.float32
    )


def layer_forward(layer_in, w_down, w_up):
    normed_f, factor = norm_rows(layer_in)
    pre = jnp.dot(normed_f.astype(jnp.bfloat16), w_down, preferred_element_type=jnp.float32)
    act = jax.nn.silu(pre).astype(jnp.bfloat16)
    out = (
        layer_in.astype(jnp.float32) + jnp.dot(act, w_up, preferred_element_type=jnp.float32)
    ).astype(jnp.bfloat16)
    return (out, pre, act)


def layer_backward(layer_in, pre, grad_out, w_down, w_up):
    normed_f, factor = norm_rows(layer_in)
    grad_act = contract_last(grad_out, w_up)
    sigma = jax.nn.sigmoid(pre)
    grad_pre = (grad_act * sigma * (1.0 + pre * (1.0 - sigma))).astype(jnp.bfloat16)
    grad_norm = contract_last(grad_pre, w_down)
    inner = jnp.mean(grad_norm * normed_f, axis=-1, keepdims=True)
    grad_in = (grad_out.astype(jnp.float32) + factor * (grad_norm - normed_f * inner)).astype(
        jnp.bfloat16
    )
    return (grad_in, normed_f.astype(jnp.bfloat16), grad_pre)


def value_grad(final, target_values, value_weight):
    normed_f, factor = norm_rows(final)
    value = jnp.sum(normed_f * value_weight, axis=-1)
    resid = value - target_values
    pulled = resid[..., None] * value_weight
    inner = jnp.mean(pulled * normed_f, axis=-1, keepdims=True)
    return (factor * (pulled - normed_f * inner)).astype(jnp.bfloat16)


def keep_slot(store, value, position, valid):
    former = lax.dynamic_index_in_dim(store, position, 0, keepdims=False)
    return lax.dynamic_update_index_in_dim(store, jnp.where(valid, value, former), position, 0)


def shards(inputs, targets, adapter_down, adapter_up, value_weight, returns):
    section_id = lax.axis_index("pipe")
    sections = lax.axis_size("pipe")
    w_down = adapter_down[0]
    w_up = adapter_up[0]
    micro_count, row_count, feature_count = inputs.shape
    rank_count = w_down.shape[1]
    tick_count = micro_count + sections - 1

    def forward_tick(loop_state, tick_index):
        incoming, input_keep, pre_keep, act_keep, final_keep = loop_state
        micro_index = tick_index - section_id
        valid = (micro_index >= 0) & (micro_index < micro_count)
        position = jnp.clip(micro_index, 0, micro_count - 1)
        fresh = lax.dynamic_index_in_dim(inputs, position, 0, keepdims=False)
        layer_in = jnp.where(section_id == 0, fresh, incoming)
        out, pre, act = layer_forward(layer_in, w_down, w_up)
        input_keep = keep_slot(input_keep, layer_in, position, valid)
        pre_keep = keep_slot(pre_keep, pre, position, valid)
        act_keep = keep_slot(act_keep, act, position, valid)
        final_keep = keep_slot(final_keep, out, position, valid)
        incoming = from_behind(out, "pipe", 1)
        return ((incoming, input_keep, pre_keep, act_keep, final_keep), None)

    start_state = (
        jnp.zeros((row_count, feature_count), jnp.bfloat16),
        jnp.zeros_like(inputs),
        jnp.zeros((micro_count, row_count, rank_count), jnp.float32),
        jnp.zeros((micro_count, row_count, rank_count), jnp.bfloat16),
        jnp.zeros_like(inputs),
    )
    forward_state, unused = lax.scan(
        forward_tick, start_state, jnp.arange(tick_count, dtype=jnp.int32)
    )
    input_keep, pre_keep, act_keep, final_keep = (
        forward_state[1],
        forward_state[2],
        forward_state[3],
        forward_state[4],
    )
    agent_ids = jnp.arange(returns.shape[0], dtype=jnp.int32)
    target_values = jnp.sum(jnp.where(targets[..., None] == agent_ids, returns, 0.0), axis=-1)
    grad_final = value_grad(final_keep, target_values, value_weight)

    def backward_tick(loop_state, tick_index):
        incoming, pre_grad_keep, out_grad_keep, sum_down, sum_up = loop_state
        micro_index = tick_index - (sections - 1 - section_id)
        valid = (micro_index >= 0) & (micro_index < micro_count)
        position = jnp.clip(micro_index, 0, micro_count - 1)
        seeded = lax.dynamic_index_in_dim(grad_final, position, 0, keepdims=False)
        grad_out = jnp.where(section_id == sections - 1, seeded, incoming)
        layer_in = lax.dynamic_index_in_dim(input_keep, position, 0, keepdims=False)
        pre = lax.dynamic_index_in_dim(pre_keep, position, 0, keepdims=False)
        act = lax.dynamic_index_in_dim(act_keep, position, 0, keepdims=False)
        grad_in, normed, grad_pre = layer_backward(layer_in, pre, grad_out, w_down, w_up)
        pre_grad_keep = keep_slot(pre_grad_keep, grad_pre, position, valid)
        out_grad_keep = keep_slot(out_grad_keep, grad_out, position, valid)

        def add_terms(sums):
            return (
                sums[0] + contract_rows(normed, grad_pre),
                sums[1] + contract_rows(grad_out, act),
            )

        def same_terms(sums):
            return sums

        sum_down, sum_up = lax.cond(valid, add_terms, same_terms, (sum_down, sum_up))
        incoming = from_behind(grad_in, "pipe", -1)
        return ((incoming, pre_grad_keep, out_grad_keep, sum_down, sum_up), None)

    zero_sum = jnp.zeros((feature_count, rank_count), jnp.float32)
    back_start = (
        jnp.zeros((row_count, feature_count), jnp.bfloat16),
        jnp.zeros((micro_count, row_count, rank_count), jnp.bfloat16),
        jnp.zeros_like(inputs),
        zero_sum,
        zero_sum,
    )
    back_state, unused = lax.scan(
        backward_tick, back_start, jnp.arange(tick_count, dtype=jnp.int32)
    )
    pre_grad_keep, out_grad_keep, sum_down, sum_up = (
        back_state[1],
        back_state[2],
        back_state[3],
        back_state[4],
    )
    down_part, up_part = (
        lax.psum_scatter(
            sum_down.astype(jnp.bfloat16), "dp", scatter_dimension=0, tiled=True
        ).astype(jnp.float32),
        lax.psum_scatter(sum_up.astype(jnp.bfloat16), "dp", scatter_dimension=0, tiled=True).astype(
            jnp.float32
        ),
    )
    return (down_part[None], up_part.T[None])


def solution(mesh):
    return jax.shard_map(
        shards,
        mesh=mesh,
        in_specs=(
            P(None, "dp", None),
            P(None, "dp"),
            P("pipe", None, None),
            P("pipe", None, None),
            P(),
            P(),
        ),
        out_specs=(P("pipe", "dp", None), P("pipe", None, "dp")),
        check_vma=False,
    )
```

profile of v0, /device:TPU:0, one launch (start us, length us, event | category | flops | bytes accessed | tf_op | source)
XLA Modules:
  0.0 928.8 jit_solution(12734150924344814036)
XLA Ops:
  12.2 366.9 %while.35 = (s32[]{:T(128)}, bf16[64,8192]{1,0:T(8,128)(2,1)S(1)}, bf16[4,64,8192]{2,1,0:T(8,128)(2,1)}, f32[4,64,256]{2,1,0:T(8,128)S(1)}, bf16[4,64,256]{2,1,0...) while((s32[]{:T(128)}, bf16[64,8192]{1,0:T(8,128)(2,1)S(1)}, ...), condition=%wide.region_2.3_spmd, body=%wide.region_0.2_spmd.sunk | while | flops 543359040 | bytes 62457944 | solution.py:99
  26.1 22.3 %collective-permute-done = bf16[64,8192]{1,0:T(8,128)(2,1)S(1)} collective-permute-done((bf16[64,8192]{1,0:T(8,128)(2,1)S(1)}, bf16[64,8192]{1,0:T(8,128)(2,1)S(1)}, u32[]{:S(2)}, u32[]{:S(2)}) %collective-permute-start) | collective-permute-done | bytes 1048608 | tf_op jit(solution)/shard_map/while/body/eval_jaxpr/ppermute | solution.py:10
  63.0 21.4 %collective-permute-done = bf16[64,8192]{1,0:T(8,128)(2,1)S(1)} collective-permute-done((bf16[64,8192]{1,0:T(8,128)(2,1)S(1)}, bf16[64,8192]{1,0:T(8,128)(2,1)S(1)}, u32[]{:S(2)}, u32[]{:S(2)}) %collective-permute-start) | collective-permute-done | bytes 1048608 | tf_op jit(solution)/shard_map/while/body/eval_jaxpr/ppermute | solution.py:10
  99.2 20.5 %collective-permute-done = bf16[64,8192]{1,0:T(8,128)(2,1)S(1)} collective-permute-done((bf16[64,8192]{1,0:T(8,128)(2,1)S(1)}, bf16[64,8192]{1,0:T(8,128)(2,1)S(1)}, u32[]{:S(2)}, u32[]{:S(2)}) %collective-permute-start) | collective-permute-done | bytes 1048608 | tf_op jit(solution)/shard_map/while/body/eval_jaxpr/ppermute | solution.py:10
  134.4 19.5 %collective-permute-done = bf16[64,8192]{1,0:T(8,128)(2,1)S(1)} collective-permute-done((bf16[64,8192]{1,0:T(8,128)(2,1)S(1)}, bf16[64,8192]{1,0:T(8,128)(2,1)S(1)}, u32[]{:S(2)}, u32[]{:S(2)}) %collective-permute-start) | collective-permute-done | bytes 1048608 | tf_op jit(solution)/shard_map/while/body/eval_jaxpr/ppermute | solution.py:10
  168.6 18.6 %collective-permute-done = bf16[64,8192]{1,0:T(8,128)(2,1)S(1)} collective-permute-done((bf16[64,8192]{1,0:T(8,128)(2,1)S(1)}, bf16[64,8192]{1,0:T(8,128)(2,1)S(1)}, u32[]{:S(2)}, u32[]{:S(2)}) %collective-permute-start) | collective-permute-done | bytes 1048608 | tf_op jit(solution)/shard_map/while/body/eval_jaxpr/ppermute | solution.py:10
  202.7 17.7 %collective-permute-done = bf16[64,8192]{1,0:T(8,128)(2,1)S(1)} collective-permute-done((bf16[64,8192]{1,0:T(8,128)(2,1)S(1)}, bf16[64,8192]{1,0:T(8,128)(2,1)S(1)}, u32[]{:S(2)}, u32[]{:S(2)}) %collective-permute-start) | collective-permute-done | bytes 1048608 | tf_op jit(solution)/shard_map/while/body/eval_jaxpr/ppermute | solution.py:10
  237.2 16.8 %collective-permute-done = bf16[64,8192]{1,0:T(8,128)(2,1)S(1)} collective-permute-done((bf16[64,8192]{1,0:T(8,128)(2,1)S(1)}, bf16[64,8192]{1,0:T(8,128)(2,1)S(1)}, u32[]{:S(2)}, u32[]{:S(2)}) %collective-permute-start) | collective-permute-done | bytes 1048608 | tf_op jit(solution)/shard_map/while/body/eval_jaxpr/ppermute | solution.py:10
  270.7 15.9 %collective-permute-done = bf16[64,8192]{1,0:T(8,128)(2,1)S(1)} collective-permute-done((bf16[64,8192]{1,0:T(8,128)(2,1)S(1)}, bf16[64,8192]{1,0:T(8,128)(2,1)S(1)}, u32[]{:S(2)}, u32[]{:S(2)}) %collective-permute-start) | collective-permute-done | bytes 1048608 | tf_op jit(solution)/shard_map/while/body/eval_jaxpr/ppermute | solution.py:10
  296.8 6.6 collective-permute-start
  303.4 15.0 %collective-permute-done = bf16[64,8192]{1,0:T(8,128)(2,1)S(1)} collective-permute-done((bf16[64,8192]{1,0:T(8,128)(2,1)S(1)}, bf16[64,8192]{1,0:T(8,128)(2,1)S(1)}, u32[]{:S(2)}, u32[]{:S(2)}) %collective-permute-start) | collective-permute-done | bytes 1048608 | tf_op jit(solution)/shard_map/while/body/eval_jaxpr/ppermute | solution.py:10
  328.6 6.6 collective-permute-start
  335.2 14.0 %collective-permute-done = bf16[64,8192]{1,0:T(8,128)(2,1)S(1)} collective-permute-done((bf16[64,8192]{1,0:T(8,128)(2,1)S(1)}, bf16[64,8192]{1,0:T(8,128)(2,1)S(1)}, u32[]{:S(2)}, u32[]{:S(2)}) %collective-permute-start) | collective-permute-done | bytes 1048608 | tf_op jit(solution)/shard_map/while/body/eval_jaxpr/ppermute | solution.py:10
  366.0 13.1 %collective-permute-done = bf16[64,8192]{1,0:T(8,128)(2,1)S(1)} collective-permute-done((bf16[64,8192]{1,0:T(8,128)(2,1)S(1)}, bf16[64,8192]{1,0:T(8,128)(2,1)S(1)}, u32[]{:S(2)}, u32[]{:S(2)}) %collective-permute-start) | collective-permute-done | bytes 1048608 | tf_op jit(solution)/shard_map/while/body/eval_jaxpr/ppermute | solution.py:10
  397.0 341.8 %while.36 = (s32[]{:T(128)}, bf16[64,8192]{1,0:T(8,128)(2,1)S(1)}, f32[8192,256]{1,0:T(8,128)}, f32[8192,256]{0,1:T(8,128)}, pred[]{:T(512)}, /*index=5*/s32[11]...) while((s32[]{:T(128)}, bf16[64,8192]{1,0:T(8,128)(2,1)S(1)}, ...), condition=%wide.region_12.13_spmd, body=%wide.region_7.12_spmd.sunk | while | flops 1086996480 | bytes 163777776 | solution.py:147
  409.8 18.4 %collective-permute-done.1 = bf16[64,8192]{1,0:T(8,128)(2,1)S(1)} collective-permute-done((bf16[64,8192]{1,0:T(8,128)(2,1)}, bf16[64,8192]{1,0:T(8,128)(2,1)S(1)}, u32[]{:S(2)}, u32[]{:S(2)}) %collective-permute-start.1) | collective-permute-done | bytes 1048608 | tf_op jit(solution)/shard_map/while/body/eval_jaxpr/ppermute | solution.py:10
  441.1 18.2 %collective-permute-done.1 = bf16[64,8192]{1,0:T(8,128)(2,1)S(1)} collective-permute-done((bf16[64,8192]{1,0:T(8,128)(2,1)}, bf16[64,8192]{1,0:T(8,128)(2,1)S(1)}, u32[]{:S(2)}, u32[]{:S(2)}) %collective-permute-start.1) | collective-permute-done | bytes 1048608 | tf_op jit(solution)/shard_map/while/body/eval_jaxpr/ppermute | solution.py:10
  472.1 18.1 %collective-permute-done.1 = bf16[64,8192]{1,0:T(8,128)(2,1)S(1)} collective-permute-done((bf16[64,8192]{1,0:T(8,128)(2,1)}, bf16[64,8192]{1,0:T(8,128)(2,1)S(1)}, u32[]{:S(2)}, u32[]{:S(2)}) %collective-permute-start.1) | collective-permute-done | bytes 1048608 | tf_op jit(solution)/shard_map/while/body/eval_jaxpr/ppermute | solution.py:10
  503.0 18.2 %collective-permute-done.1 = bf16[64,8192]{1,0:T(8,128)(2,1)S(1)} collective-permute-done((bf16[64,8192]{1,0:T(8,128)(2,1)}, bf16[64,8192]{1,0:T(8,128)(2,1)S(1)}, u32[]{:S(2)}, u32[]{:S(2)}) %collective-permute-start.1) | collective-permute-done | bytes 1048608 | tf_op jit(solution)/shard_map/while/body/eval_jaxpr/ppermute | solution.py:10
  534.0 17.7 %collective-permute-done.1 = bf16[64,8192]{1,0:T(8,128)(2,1)S(1)} collective-permute-done((bf16[64,8192]{1,0:T(8,128)(2,1)}, bf16[64,8192]{1,0:T(8,128)(2,1)S(1)}, u32[]{:S(2)}, u32[]{:S(2)}) %collective-permute-start.1) | collective-permute-done | bytes 1048608 | tf_op jit(solution)/shard_map/while/body/eval_jaxpr/ppermute | solution.py:10
  564.5 17.7 %collective-permute-done.1 = bf16[64,8192]{1,0:T(8,128)(2,1)S(1)} collective-permute-done((bf16[64,8192]{1,0:T(8,128)(2,1)}, bf16[64,8192]{1,0:T(8,128)(2,1)S(1)}, u32[]{:S(2)}, u32[]{:S(2)}) %collective-permute-start.1) | collective-permute-done | bytes 1048608 | tf_op jit(solution)/shard_map/while/body/eval_jaxpr/ppermute | solution.py:10
  595.0 17.7 %collective-permute-done.1 = bf16[64,8192]{1,0:T(8,128)(2,1)S(1)} collective-permute-done((bf16[64,8192]{1,0:T(8,128)(2,1)}, bf16[64,8192]{1,0:T(8,128)(2,1)S(1)}, u32[]{:S(2)}, u32[]{:S(2)}) %collective-permute-start.1) | collective-permute-done | bytes 1048608 | tf_op jit(solution)/shard_map/while/body/eval_jaxpr/ppermute | solution.py:10
  625.5 14.1 %conditional.2 = ((f32[8192,256]{1,0:T(8,128)}, f32[8192,256]{0,1:T(8,128)})) conditional(s32[]{:T(128)} %convert_element_type.130, (f32[8192,256]{1,0:T(8,128)}, f32[8192,256]{0,1:T(8,128)}) %tuple.75, (bf16[64,8192]{1,0:T(8,128)(2,1)S(1)}, bf16[64,256]{1,0:T(8,128)(2,1)S(1)}, f32[8192,256]{1,0:T(8,128)}, bf16[4,64,256]{2,1,0:T(8,128)(2,1)}, ...), branch_computations={%region_10.10_spmd, %region_11.11_spmd} | conditional | flops 541065216 | bytes 102826576 | solution.py:135
  625.5 8.0 convolution_add_fusion.1
  656.0 14.1 %conditional.2 = ((f32[8192,256]{1,0:T(8,128)}, f32[8192,256]{0,1:T(8,128)})) conditional(s32[]{:T(128)} %convert_element_type.130, (f32[8192,256]{1,0:T(8,128)}, f32[8192,256]{0,1:T(8,128)}) %tuple.75, (bf16[64,8192]{1,0:T(8,128)(2,1)S(1)}, bf16[64,256]{1,0:T(8,128)(2,1)S(1)}, f32[8192,256]{1,0:T(8,128)}, bf16[4,64,256]{2,1,0:T(8,128)(2,1)}, ...), branch_computations={%region_10.10_spmd, %region_11.11_spmd} | conditional | flops 541065216 | bytes 102826576 | solution.py:135
  656.0 8.0 convolution_add_fusion.1
  687.3 14.1 %conditional.2 = ((f32[8192,256]{1,0:T(8,128)}, f32[8192,256]{0,1:T(8,128)})) conditional(s32[]{:T(128)} %convert_element_type.130, (f32[8192,256]{1,0:T(8,128)}, f32[8192,256]{0,1:T(8,128)}) %tuple.75, (bf16[64,8192]{1,0:T(8,128)(2,1)S(1)}, bf16[64,256]{1,0:T(8,128)(2,1)S(1)}, f32[8192,256]{1,0:T(8,128)}, bf16[4,64,256]{2,1,0:T(8,128)(2,1)}, ...), branch_computations={%region_10.10_spmd, %region_11.11_spmd} | conditional | flops 541065216 | bytes 102826576 | solution.py:135
  687.4 8.1 convolution_add_fusion.1
  720.3 14.1 %conditional.2 = ((f32[8192,256]{1,0:T(8,128)}, f32[8192,256]{0,1:T(8,128)})) conditional(s32[]{:T(128)} %convert_element_type.130, (f32[8192,256]{1,0:T(8,128)}, f32[8192,256]{0,1:T(8,128)}) %tuple.75, (bf16[64,8192]{1,0:T(8,128)(2,1)S(1)}, bf16[64,256]{1,0:T(8,128)(2,1)S(1)}, f32[8192,256]{1,0:T(8,128)}, bf16[4,64,256]{2,1,0:T(8,128)(2,1)}, ...), branch_computations={%region_10.10_spmd, %region_11.11_spmd} | conditional | flops 541065216 | bytes 102826576 | solution.py:135
  720.3 8.0 convolution_add_fusion.1
  750.5 85.6 %reduce-scatter.3.cloned.1.call-done = bf16[512,256]{1,0:T(8,128)(2,1)} async-done(((bf16[8192,256]{1,0:T(8,128)(2,1)}), bf16[512,256]{1,0:T(8,128)(2,1)}) %reduce-scatter.3.cloned.1.call-update) | async-done | bytes 262160 | tf_op jit(solution)/shard_map/reduce_scatter | solution.py:157
  837.9 82.3 %reduce-scatter.5.cloned.1.call-done = bf16[512,256]{0,1:T(8,128)(2,1)} async-done(((bf16[8192,256]{0,1:T(8,128)(2,1)}), bf16[512,256]{0,1:T(8,128)(2,1)}) %reduce-scatter.5.cloned.1.call-update) | async-done | bytes 262160 | tf_op jit(solution)/shard_map/reduce_scatter | solution.py:160
  (373 shorter events, 365.0 us)
Async XLA Ops:
  7.2 828.9 %reduce-scatter.3.cloned.1.call-start = ((), (), s32[]{:S(2)}) async-start(), calls=%async_computation.2 | async-start | bytes 4456448 | tf_op jit(solution)/shard_map/reduce_scatter | solution.py:157
  12.2 370.4 %copy-start.8 = (f32[8192]{0:T(1024)S(1)}, f32[8192]{0:T(1024)}, u32[]{:S(2)}) copy-start(f32[8192]{0:T(1024)} %param.16) | copy-start | bytes 98308
  22.4 26.0 %collective-permute-start = (bf16[64,8192]{1,0:T(8,128)(2,1)S(1)}, bf16[64,8192]{1,0:T(8,128)(2,1)S(1)}, u32[]{:S(2)}, u32[]{:S(2)}) collective-permute-start(bf16[64,8192]{1,0:T(8,128)(2,1)S(1)} %get-tuple-element.549), channel_id=1, source_target_pairs={{0,1},{1,2},{2,3},{3,4},{4,5},{5,6},{6,7},{8,9},{9,10},{10,11},{11... | collective-permute-start | bytes 3145736 | tf_op jit(solution)/shard_map/while/body/eval_jaxpr/ppermute | solution.py:10
  58.6 25.8 %collective-permute-start = (bf16[64,8192]{1,0:T(8,128)(2,1)S(1)}, bf16[64,8192]{1,0:T(8,128)(2,1)S(1)}, u32[]{:S(2)}, u32[]{:S(2)}) collective-permute-start(bf16[64,8192]{1,0:T(8,128)(2,1)S(1)} %get-tuple-element.549), channel_id=1, source_target_pairs={{0,1},{1,2},{2,3},{3,4},{4,5},{5,6},{6,7},{8,9},{9,10},{10,11},{11... | collective-permute-start | bytes 3145736 | tf_op jit(solution)/shard_map/while/body/eval_jaxpr/ppermute | solution.py:10
  87.1 3.5 copy-start
  94.6 25.0 %collective-permute-start = (bf16[64,8192]{1,0:T(8,128)(2,1)S(1)}, bf16[64,8192]{1,0:T(8,128)(2,1)S(1)}, u32[]{:S(2)}, u32[]{:S(2)}) collective-permute-start(bf16[64,8192]{1,0:T(8,128)(2,1)S(1)} %get-tuple-element.549), channel_id=1, source_target_pairs={{0,1},{1,2},{2,3},{3,4},{4,5},{5,6},{6,7},{8,9},{9,10},{10,11},{11... | collective-permute-start | bytes 3145736 | tf_op jit(solution)/shard_map/while/body/eval_jaxpr/ppermute | solution.py:10
  129.8 24.1 %collective-permute-start = (bf16[64,8192]{1,0:T(8,128)(2,1)S(1)}, bf16[64,8192]{1,0:T(8,128)(2,1)S(1)}, u32[]{:S(2)}, u32[]{:S(2)}) collective-permute-start(bf16[64,8192]{1,0:T(8,128)(2,1)S(1)} %get-tuple-element.549), channel_id=1, source_target_pairs={{0,1},{1,2},{2,3},{3,4},{4,5},{5,6},{6,7},{8,9},{9,10},{10,11},{11... | collective-permute-start | bytes 3145736 | tf_op jit(solution)/shard_map/while/body/eval_jaxpr/ppermute | solution.py:10
  164.1 23.1 %collective-permute-start = (bf16[64,8192]{1,0:T(8,128)(2,1)S(1)}, bf16[64,8192]{1,0:T(8,128)(2,1)S(1)}, u32[]{:S(2)}, u32[]{:S(2)}) collective-permute-start(bf16[64,8192]{1,0:T(8,128)(2,1)S(1)} %get-tuple-element.549), channel_id=1, source_target_pairs={{0,1},{1,2},{2,3},{3,4},{4,5},{5,6},{6,7},{8,9},{9,10},{10,11},{11... | collective-permute-start | bytes 3145736 | tf_op jit(solution)/shard_map/while/body/eval_jaxpr/ppermute | solution.py:10
  197.4 23.0 %collective-permute-start = (bf16[64,8192]{1,0:T(8,128)(2,1)S(1)}, bf16[64,8192]{1,0:T(8,128)(2,1)S(1)}, u32[]{:S(2)}, u32[]{:S(2)}) collective-permute-start(bf16[64,8192]{1,0:T(8,128)(2,1)S(1)} %get-tuple-element.549), channel_id=1, source_target_pairs={{0,1},{1,2},{2,3},{3,4},{4,5},{5,6},{6,7},{8,9},{9,10},{10,11},{11... | collective-permute-start | bytes 3145736 | tf_op jit(solution)/shard_map/while/body/eval_jaxpr/ppermute | solution.py:10
  230.6 23.4 %collective-permute-start = (bf16[64,8192]{1,0:T(8,128)(2,1)S(1)}, bf16[64,8192]{1,0:T(8,128)(2,1)S(1)}, u32[]{:S(2)}, u32[]{:S(2)}) collective-permute-start(bf16[64,8192]{1,0:T(8,128)(2,1)S(1)} %get-tuple-element.549), channel_id=1, source_target_pairs={{0,1},{1,2},{2,3},{3,4},{4,5},{5,6},{6,7},{8,9},{9,10},{10,11},{11... | collective-permute-start | bytes 3145736 | tf_op jit(solution)/shard_map/while/body/eval_jaxpr/ppermute | solution.py:10
  264.1 22.5 %collective-permute-start = (bf16[64,8192]{1,0:T(8,128)(2,1)S(1)}, bf16[64,8192]{1,0:T(8,128)(2,1)S(1)}, u32[]{:S(2)}, u32[]{:S(2)}) collective-permute-start(bf16[64,8192]{1,0:T(8,128)(2,1)S(1)} %get-tuple-element.549), channel_id=1, source_target_pairs={{0,1},{1,2},{2,3},{3,4},{4,5},{5,6},{6,7},{8,9},{9,10},{10,11},{11... | collective-permute-start | bytes 3145736 | tf_op jit(solution)/shard_map/while/body/eval_jaxpr/ppermute | solution.py:10
  296.8 21.6 %collective-permute-start = (bf16[64,8192]{1,0:T(8,128)(2,1)S(1)}, bf16[64,8192]{1,0:T(8,128)(2,1)S(1)}, u32[]{:S(2)}, u32[]{:S(2)}) collective-permute-start(bf16[64,8192]{1,0:T(8,128)(2,1)S(1)} %get-tuple-element.549), channel_id=1, source_target_pairs={{0,1},{1,2},{2,3},{3,4},{4,5},{5,6},{6,7},{8,9},{9,10},{10,11},{11... | collective-permute-start | bytes 3145736 | tf_op jit(solution)/shard_map/while/body/eval_jaxpr/ppermute | solution.py:10
  328.6 20.7 %collective-permute-start = (bf16[64,8192]{1,0:T(8,128)(2,1)S(1)}, bf16[64,8192]{1,0:T(8,128)(2,1)S(1)}, u32[]{:S(2)}, u32[]{:S(2)}) collective-permute-start(bf16[64,8192]{1,0:T(8,128)(2,1)S(1)} %get-tuple-element.549), channel_id=1, source_target_pairs={{0,1},{1,2},{2,3},{3,4},{4,5},{5,6},{6,7},{8,9},{9,10},{10,11},{11... | collective-permute-start | bytes 3145736 | tf_op jit(solution)/shard_map/while/body/eval_jaxpr/ppermute | solution.py:10
  359.4 19.7 %collective-permute-start = (bf16[64,8192]{1,0:T(8,128)(2,1)S(1)}, bf16[64,8192]{1,0:T(8,128)(2,1)S(1)}, u32[]{:S(2)}, u32[]{:S(2)}) collective-permute-start(bf16[64,8192]{1,0:T(8,128)(2,1)S(1)} %get-tuple-element.549), channel_id=1, source_target_pairs={{0,1},{1,2},{2,3},{3,4},{4,5},{5,6},{6,7},{8,9},{9,10},{10,11},{11... | collective-permute-start | bytes 3145736 | tf_op jit(solution)/shard_map/while/body/eval_jaxpr/ppermute | solution.py:10
  379.1 4.9 copy-start.7
  379.1 3.5 copy-start.6
  408.5 19.8 %collective-permute-start.1 = (bf16[64,8192]{1,0:T(8,128)(2,1)}, bf16[64,8192]{1,0:T(8,128)(2,1)S(1)}, u32[]{:S(2)}, u32[]{:S(2)}) collective-permute-start(bf16[64,8192]{1,0:T(8,128)(2,1)} %get-tuple-element.568), channel_id=1, source_target_pairs={{1,0},{2,1},{3,2},{4,3},{5,4},{6,5},{7,6},{9,8},{10,9},{11,10},{12... | collective-permute-start | bytes 3145736 | tf_op jit(solution)/shard_map/while/body/eval_jaxpr/ppermute | solution.py:10
  439.8 19.5 %collective-permute-start.1 = (bf16[64,8192]{1,0:T(8,128)(2,1)}, bf16[64,8192]{1,0:T(8,128)(2,1)S(1)}, u32[]{:S(2)}, u32[]{:S(2)}) collective-permute-start(bf16[64,8192]{1,0:T(8,128)(2,1)} %get-tuple-element.568), channel_id=1, source_target_pairs={{1,0},{2,1},{3,2},{4,3},{5,4},{6,5},{7,6},{9,8},{10,9},{11,10},{12... | collective-permute-start | bytes 3145736 | tf_op jit(solution)/shard_map/while/body/eval_jaxpr/ppermute | solution.py:10
  470.7 19.5 %collective-permute-start.1 = (bf16[64,8192]{1,0:T(8,128)(2,1)}, bf16[64,8192]{1,0:T(8,128)(2,1)S(1)}, u32[]{:S(2)}, u32[]{:S(2)}) collective-permute-start(bf16[64,8192]{1,0:T(8,128)(2,1)} %get-tuple-element.568), channel_id=1, source_target_pairs={{1,0},{2,1},{3,2},{4,3},{5,4},{6,5},{7,6},{9,8},{10,9},{11,10},{12... | collective-permute-start | bytes 3145736 | tf_op jit(solution)/shard_map/while/body/eval_jaxpr/ppermute | solution.py:10
  501.7 19.5 %collective-permute-start.1 = (bf16[64,8192]{1,0:T(8,128)(2,1)}, bf16[64,8192]{1,0:T(8,128)(2,1)S(1)}, u32[]{:S(2)}, u32[]{:S(2)}) collective-permute-start(bf16[64,8192]{1,0:T(8,128)(2,1)} %get-tuple-element.568), channel_id=1, source_target_pairs={{1,0},{2,1},{3,2},{4,3},{5,4},{6,5},{7,6},{9,8},{10,9},{11,10},{12... | collective-permute-start | bytes 3145736 | tf_op jit(solution)/shard_map/while/body/eval_jaxpr/ppermute | solution.py:10
  532.7 19.0 %collective-permute-start.1 = (bf16[64,8192]{1,0:T(8,128)(2,1)}, bf16[64,8192]{1,0:T(8,128)(2,1)S(1)}, u32[]{:S(2)}, u32[]{:S(2)}) collective-permute-start(bf16[64,8192]{1,0:T(8,128)(2,1)} %get-tuple-element.568), channel_id=1, source_target_pairs={{1,0},{2,1},{3,2},{4,3},{5,4},{6,5},{7,6},{9,8},{10,9},{11,10},{12... | collective-permute-start | bytes 3145736 | tf_op jit(solution)/shard_map/while/body/eval_jaxpr/ppermute | solution.py:10
  563.2 19.0 %collective-permute-start.1 = (bf16[64,8192]{1,0:T(8,128)(2,1)}, bf16[64,8192]{1,0:T(8,128)(2,1)S(1)}, u32[]{:S(2)}, u32[]{:S(2)}) collective-permute-start(bf16[64,8192]{1,0:T(8,128)(2,1)} %get-tuple-element.568), channel_id=1, source_target_pairs={{1,0},{2,1},{3,2},{4,3},{5,4},{6,5},{7,6},{9,8},{10,9},{11,10},{12... | collective-permute-start | bytes 3145736 | tf_op jit(solution)/shard_map/while/body/eval_jaxpr/ppermute | solution.py:10
  593.7 19.0 %collective-permute-start.1 = (bf16[64,8192]{1,0:T(8,128)(2,1)}, bf16[64,8192]{1,0:T(8,128)(2,1)S(1)}, u32[]{:S(2)}, u32[]{:S(2)}) collective-permute-start(bf16[64,8192]{1,0:T(8,128)(2,1)} %get-tuple-element.568), channel_id=1, source_target_pairs={{1,0},{2,1},{3,2},{4,3},{5,4},{6,5},{7,6},{9,8},{10,9},{11,10},{12... | collective-permute-start | bytes 3145736 | tf_op jit(solution)/shard_map/while/body/eval_jaxpr/ppermute | solution.py:10
  624.2 19.0 %collective-permute-start.1 = (bf16[64,8192]{1,0:T(8,128)(2,1)}, bf16[64,8192]{1,0:T(8,128)(2,1)S(1)}, u32[]{:S(2)}, u32[]{:S(2)}) collective-permute-start(bf16[64,8192]{1,0:T(8,128)(2,1)} %get-tuple-element.568), channel_id=1, source_target_pairs={{1,0},{2,1},{3,2},{4,3},{5,4},{6,5},{7,6},{9,8},{10,9},{11,10},{12... | collective-permute-start | bytes 3145736 | tf_op jit(solution)/shard_map/while/body/eval_jaxpr/ppermute | solution.py:10
  625.5 8.1 copy-start.4
  654.7 19.9 %collective-permute-start.1 = (bf16[64,8192]{1,0:T(8,128)(2,1)}, bf16[64,8192]{1,0:T(8,128)(2,1)S(1)}, u32[]{:S(2)}, u32[]{:S(2)}) collective-permute-start(bf16[64,8192]{1,0:T(8,128)(2,1)} %get-tuple-element.568), channel_id=1, source_target_pairs={{1,0},{2,1},{3,2},{4,3},{5,4},{6,5},{7,6},{9,8},{10,9},{11,10},{12... | collective-permute-start | bytes 3145736 | tf_op jit(solution)/shard_map/while/body/eval_jaxpr/ppermute | solution.py:10
  656.0 8.1 copy-start.4
  686.0 21.5 %collective-permute-start.1 = (bf16[64,8192]{1,0:T(8,128)(2,1)}, bf16[64,8192]{1,0:T(8,128)(2,1)S(1)}, u32[]{:S(2)}, u32[]{:S(2)}) collective-permute-start(bf16[64,8192]{1,0:T(8,128)(2,1)} %get-tuple-element.568), channel_id=1, source_target_pairs={{1,0},{2,1},{3,2},{4,3},{5,4},{6,5},{7,6},{9,8},{10,9},{11,10},{12... | collective-permute-start | bytes 3145736 | tf_op jit(solution)/shard_map/while/body/eval_jaxpr/ppermute | solution.py:10
  687.3 8.1 copy-start.4
  719.0 19.8 %collective-permute-start.1 = (bf16[64,8192]{1,0:T(8,128)(2,1)}, bf16[64,8192]{1,0:T(8,128)(2,1)S(1)}, u32[]{:S(2)}, u32[]{:S(2)}) collective-permute-start(bf16[64,8192]{1,0:T(8,128)(2,1)} %get-tuple-element.568), channel_id=1, source_target_pairs={{1,0},{2,1},{3,2},{4,3},{5,4},{6,5},{7,6},{9,8},{10,9},{11,10},{12... | collective-permute-start | bytes 3145736 | tf_op jit(solution)/shard_map/while/body/eval_jaxpr/ppermute | solution.py:10
  720.3 8.1 copy-start.4
  744.6 175.6 %reduce-scatter.5.cloned.1.call-start = ((), (), s32[]{:S(2)}) async-start(), calls=%async_computation.3 | async-start | bytes 4456448 | tf_op jit(solution)/shard_map/reduce_scatter | solution.py:160
  (49 other events, 145.9 us)
Sparse Core Ops, SparseCore 0:
  744.7 91.3 reduce-scatter.2
  840.6 79.4 reduce-scatter.4
where the time goes:
time: 932 us; the launch traced here: 929 us
  waiting for transfers between devices  507 us (54%)
  other arithmetic  131 us (14%)
  matrix products  122 us (13%)
  starting transfers between devices  73.5 us (8%)
  local copies, waits for them, and re-layouts  64.9 us (7%)
  loops' own time  15.8 us (2%)
  between operations  14.1 us (2%)
    ppermute x22, waiting for transfers between devices, from_behind(): lax.ppermute(value, axis, [(source, source + steps) for source in range(f...  339 us
    reduce_scatter x1, waiting for transfers between devices, shards(): lax.psum_scatter(sum_down.astype(jnp.bfloat16), 'dp', scatter_dimension=0...  85.6 us
    reduce_scatter x1, waiting for transfers between devices, shards(): lax.psum_scatter(sum_up.astype(jnp.bfloat16), 'dp', scatter_dimension=0,...  82.3 us
    ppermute x22, starting transfers between devices, from_behind(): lax.ppermute(value, axis, [(source, source + steps) for source in range(f...  73.4 us
    dot_general x22, matrix products, contract_last(): lax.dot_general(left, right, (((1,), (1,)), ((), ())), preferred_element_...  45.6 us
    dot_general x8, matrix products, contract_rows(): lax.dot_general(left, right, (((0,), (0,)), ((), ())), preferred_element_...  43.2 us
    dynamic_update_slice x22, other arithmetic, keep_slot(): lax.dynamic_update_index_in_dim(store, jnp.where(valid, value, former), p...  35 us
    convert_element_type x11, other arithmetic, layer_backward(): return (grad_in, normed_f.astype(jnp.bfloat16), grad_pre)  32.3 us
  transfers between devices with their start and end apart: 24, of which 24 were waited for; matrix products, arithmetic and copies ran while one was open for 6% of the time, Pallas kernels for 0%

commit v1 on v0

v1 whole, which is shorter than its diff:
```python
import functools

import jax
import jax.numpy as jnp
from jax import lax
from jax.experimental import pallas as pl
from jax.experimental.pallas import tpu as pltpu
from jax.sharding import PartitionSpec as P

LAYERS = 8
ZN = 4
TOK = 128
OWN = TOK // ZN
CH = 2048
RANK = 256
FEAT = 8192
TILE = 512
F32 = jnp.float32
BF16 = jnp.bfloat16
MESH = pl.DeviceIdType.MESH


def split3(row):
    hi = row.astype(BF16)
    rest = row - hi.astype(F32)
    mid = rest.astype(BF16)
    lo = (rest - mid.astype(F32)).astype(BF16)
    return [hi.astype(F32), mid.astype(F32), lo.astype(F32)]


def pack_rows(rows):
    parts = []
    for row in rows:
        parts += split3(row)
    at = lax.broadcasted_iota(jnp.int32, (16, 128), 0)
    tile = jnp.zeros((16, 128), F32)
    for i, part in enumerate(parts):
        tile = jnp.where(at == i, jnp.broadcast_to(part, (16, 128)), tile)
    return tile.astype(BF16)


def column(row):
    return jnp.transpose(jnp.broadcast_to(row, (TOK, 128)))


def row_sums(acc):
    return jnp.sum(jnp.transpose(acc), axis=0, keepdims=True)


def fold_lanes(tile):
    total = tile[:, 0:128]
    for i in range(1, tile.shape[1] // 128):
        total = total + tile[:, 128 * i : 128 * (i + 1)]
    return total


def wide(col, width):
    return jnp.concatenate([col] * (width // 128), axis=1)


def dot(a, b):
    return lax.dot_general(a, b, (((1,), (0,)), ((), ())), preferred_element_type=F32)


def dot_nt(a, b):
    return lax.dot_general(a, b, (((1,), (1,)), ((), ())), preferred_element_type=F32)


def dot_tn(a, b):
    return lax.dot_general(a, b, (((0,), (0,)), ((), ())), preferred_element_type=F32)


def kernel(
    x_hbm, wd_hbm, wu_hbm, vw_ref, tv_ref, out_hbm,
    xs, wd, wu, snd, rcv, mine, gx, pre_s, act_s, scale_s, gbuf,
    x_ssem, x_rsem, lsem, wsem, ssem, rsem, gsem,
):
    dp = lax.axis_index("dp")
    pipe = lax.axis_index("pipe")
    z = dp // 4
    rest = lax.rem(dp, 4)
    xl = pipe // 4
    y = lax.rem(pipe, 4)
    zs = [lax.rem(z + i, ZN) for i in range(1, ZN)]
    peers = [(zz * 4 + rest, pipe) for zz in zs]

    for layer in range(LAYERS):
        pltpu.make_async_copy(wd_hbm.at[layer], wd.at[layer], wsem.at[0, layer]).start()
        pltpu.make_async_copy(wu_hbm.at[layer], wu.at[layer], wsem.at[1, layer]).start()

    def piece(zz):
        return x_hbm.at[y, pl.ds(pl.multiple_of(xl * OWN, OWN), OWN), pl.ds(pl.multiple_of(zz * CH, CH), CH)]

    own_rows = pl.ds(pl.multiple_of(z * OWN, OWN), OWN)
    own = pltpu.make_async_copy(piece(z), xs.at[0, own_rows], lsem)
    own.start()

    barrier = pltpu.get_barrier_semaphore()
    for peer in peers:
        pl.semaphore_signal(barrier, inc=1, device_id=peer, device_id_type=MESH)
    pl.semaphore_wait(barrier, ZN - 1)

    copies = []
    for i in range(ZN - 1):
        copy = pltpu.make_async_remote_copy(
            src_ref=piece(zs[i]), dst_ref=xs.at[0, own_rows],
            send_sem=x_ssem.at[i], recv_sem=x_rsem.at[i],
            device_id=peers[i], device_id_type=MESH,
        )
        copy.start()
        copies.append(copy)
    own.wait()
    for copy in copies:
        copy.wait()

    def exchange(slot, rows):
        copies = []
        for i in range(ZN - 1):
            copy = pltpu.make_async_remote_copy(
                src_ref=snd.at[slot, pl.ds(0, rows)],
                dst_ref=rcv.at[slot, i, pl.ds(0, rows)],
                send_sem=ssem.at[slot, i], recv_sem=rsem.at[slot, i],
                device_id=peers[i], device_id_type=MESH,
            )
            copy.start()
            copies.append(copy)
        return copies

    def finish(copies):
        for copy in copies:
            copy.wait()

    def wait_weights(which, layer):
        if which == 0:
            pltpu.make_async_copy(wd_hbm.at[layer], wd.at[layer], wsem.at[0, layer]).wait()
        else:
            pltpu.make_async_copy(wu_hbm.at[layer], wu.at[layer], wsem.at[1, layer]).wait()

    def cols(t):
        return slice(t * TILE, (t + 1) * TILE)

    def send_product(slot, product, square):
        mine[...] = product
        snd[slot, 16 : 16 + TOK] = product.astype(BF16)
        row = row_sums(square)
        snd[slot, 0:16, 0:128] = pack_rows([row])
        return row

    def row_total(slot, first, own_row):
        total = own_row
        for i in range(ZN - 1):
            part = rcv[slot, i, 0:16, 0:128].astype(F32)[first : first + 3]
            total = total + jnp.sum(part, axis=0, keepdims=True)
        return total

    snd[...] = jnp.zeros_like(snd)
    wait_weights(0, 0)
    product = jnp.zeros((TOK, RANK), F32)
    square = jnp.zeros((TOK, 128), F32)
    for t in range(CH // TILE):
        tile = xs[0, :, cols(t)]
        wide_tile = tile.astype(F32)
        square += fold_lanes(wide_tile * wide_tile)
        product += dot(tile, wd[0, cols(t), :])
    own_row = send_product(0, product, square)

    def forward(layer, own_row):
        slot = lax.rem(layer, 2)
        copies = exchange(slot, 16 + TOK)
        wait_weights(1, layer)
        finish(copies)
        total = mine[...]
        for i in range(ZN - 1):
            total = total + rcv[slot, i, 16 : 16 + TOK].astype(F32)
        ssq = row_total(slot, 0, own_row)
        scale = column(lax.rsqrt(ssq * (1.0 / FEAT) + 1e-05))
        pre = total * wide(scale, RANK)
        act = (pre / (1.0 + jnp.exp(-pre))).astype(BF16)
        scale_s[layer] = scale
        pre_s[layer] = pre
        act_s[layer] = act
        after = jnp.minimum(layer + 1, LAYERS - 1)

        @pl.when(layer < LAYERS - 1)
        def _():
            wait_weights(0, layer + 1)

        product = jnp.zeros((TOK, RANK), F32)
        square = jnp.zeros((TOK, 128), F32)
        for t in range(CH // TILE):
            tile = (xs[layer, :, cols(t)].astype(F32) + dot(act, wu[layer, :, cols(t)])).astype(BF16)
            xs[layer + 1, :, cols(t)] = tile
            wide_tile = tile.astype(F32)
            square += fold_lanes(wide_tile * wide_tile)
            product += dot(tile, wd[after, cols(t), :])
        return send_product(1 - slot, product, square)

    own_row = lax.fori_loop(0, LAYERS, forward, own_row)

    value_acc = jnp.zeros((TOK, 128), F32)
    for t in range(CH // TILE):
        weight = vw_ref[pl.ds(z, 1), cols(t)]
        value_acc += fold_lanes(xs[LAYERS, :, cols(t)].astype(F32) * weight)
    value_row = row_sums(value_acc)
    target_row = tv_ref[0:1, :]
    snd[0, 0:16, 0:128] = pack_rows([own_row, value_row, target_row])
    finish(exchange(0, 16))
    ssq = row_total(0, 0, own_row)
    raw = row_total(0, 3, value_row)
    target = row_total(0, 6, target_row)
    scale = lax.rsqrt(ssq * (1.0 / FEAT) + 1e-05)
    value = scale * raw
    resid = value - target
    on_weight = column(scale * resid)
    on_x = column(-scale * scale * resid * value * (1.0 / FEAT))
    product = jnp.zeros((TOK, RANK), F32)
    for t in range(CH // TILE):
        weight = vw_ref[pl.ds(z, 1), cols(t)]
        tile = (
            wide(on_weight, TILE) * weight + wide(on_x, TILE) * xs[LAYERS, :, cols(t)].astype(F32)
        ).astype(BF16)
        gx[0, :, cols(t)] = tile
        product += dot_nt(tile, wu[LAYERS - 1, :, cols(t)])
    mine[...] = product
    snd[1, 16 : 16 + TOK] = product.astype(BF16)

    def out_copy(layer, slot):
        return pltpu.make_async_copy(gbuf.at[slot], out_hbm.at[layer], gsem.at[slot])

    def backward(step, carry):
        layer = LAYERS - 1 - step
        slot = lax.rem(step + 1, 2)
        now = lax.rem(step, 2)
        finish(exchange(slot, 16 + TOK))
        total = mine[...]
        for i in range(ZN - 1):
            total = total + rcv[slot, i, 16 : 16 + TOK].astype(F32)
        pre = pre_s[layer]
        scale = scale_s[layer]
        sigma = 1.0 / (1.0 + jnp.exp(-pre))
        grad_pre = (total * sigma * (1.0 + pre * (1.0 - sigma))).astype(BF16)
        grad_f = grad_pre.astype(F32)
        inner = jnp.sum(grad_f * pre, axis=1, keepdims=True) * (1.0 / FEAT)
        scaled = (grad_f * wide(scale, RANK)).astype(BF16)
        on_x = wide(scale * scale * inner, TILE)
        on_q = wide(scale, TILE)
        below = jnp.maximum(layer - 1, 0)
        product = jnp.zeros((TOK, RANK), F32)
        for t in range(CH // TILE):
            q = dot_nt(grad_pre, wd[layer, cols(t), :])
            tile = (
                gx[now, :, cols(t)].astype(F32) + on_q * q - on_x * xs[layer, :, cols(t)].astype(F32)
            ).astype(BF16)
            gx[1 - now, :, cols(t)] = tile
            product += dot_nt(tile, wu[below, :, cols(t)])
        mine[...] = product
        snd[1 - slot, 16 : 16 + TOK] = product.astype(BF16)

        @pl.when(step >= 2)
        def _():
            out_copy(layer + 2, now).wait()

        act = act_s[layer]
        for t in range(CH // TILE):
            gbuf[now, 0:RANK, cols(t)] = dot_tn(scaled, xs[layer, :, cols(t)]).astype(BF16)
            gbuf[now, RANK : 2 * RANK, cols(t)] = dot_tn(act, gx[now, :, cols(t)]).astype(BF16)
        out_copy(layer, now).start()
        return carry

    lax.fori_loop(0, LAYERS, backward, 0)
    out_copy(1, 0).wait()
    out_copy(0, 1).wait()


def shards(inputs, targets, adapter_down, adapter_up, value_weight, returns):
    dp = lax.axis_index("dp")
    pipe = lax.axis_index("pipe")
    z = dp // 4
    xl, y = pipe // 4, pipe % 4
    down = lax.dynamic_slice_in_dim(adapter_down[0], z * CH, CH, 0)
    up = lax.dynamic_slice_in_dim(adapter_up[0], z * CH, CH, 1)
    wd = lax.all_gather(down, "pipe")
    wu = lax.all_gather(up, "pipe")
    mine = lax.dynamic_slice(targets, (y, xl * OWN), (1, OWN))
    agents = jnp.arange(returns.shape[0], dtype=jnp.int32)
    values = jnp.sum(jnp.where(mine[0][:, None] == agents, returns, 0.0), axis=-1)
    tv = lax.dynamic_update_slice(jnp.zeros((8, 128), F32), values[None], (0, z * OWN))
    any_spec = pl.BlockSpec(memory_space=pl.ANY)
    vmem = pl.BlockSpec(memory_space=pltpu.VMEM)
    part = pl.pallas_call(
        kernel,
        out_shape=jax.ShapeDtypeStruct((LAYERS, 2 * RANK, CH), BF16),
        in_specs=[any_spec, any_spec, any_spec, vmem, vmem],
        out_specs=any_spec,
        scratch_shapes=[
            pltpu.VMEM((LAYERS + 1, TOK, CH), BF16),
            pltpu.VMEM((LAYERS, CH, RANK), BF16),
            pltpu.VMEM((LAYERS, RANK, CH), BF16),
            pltpu.VMEM((2, 16 + TOK, RANK), BF16),
            pltpu.VMEM((2, ZN - 1, 16 + TOK, RANK), BF16),
            pltpu.VMEM((TOK, RANK), F32),
            pltpu.VMEM((2, TOK, CH), BF16),
            pltpu.VMEM((LAYERS, TOK, RANK), F32),
            pltpu.VMEM((LAYERS, TOK, RANK), BF16),
            pltpu.VMEM((LAYERS, TOK, 128), F32),
            pltpu.VMEM((2, 2 * RANK, CH), BF16),
            pltpu.SemaphoreType.DMA((ZN - 1,)),
            pltpu.SemaphoreType.DMA((ZN - 1,)),
            pltpu.SemaphoreType.DMA,
            pltpu.SemaphoreType.DMA((2, LAYERS)),
            pltpu.SemaphoreType.DMA((2, ZN - 1)),
            pltpu.SemaphoreType.DMA((2, ZN - 1)),
            pltpu.SemaphoreType.DMA((2,)),
        ],
        compiler_params=pltpu.CompilerParams(
            collective_id=0, has_side_effects=True, vmem_limit_bytes=56 * 1024 * 1024
        ),
        name="relay",
    )(inputs, wd, wu, value_weight.reshape(ZN, CH), tv)
    mine = lax.psum_scatter(part, "pipe", scatter_dimension=0, tiled=True)[0]
    groups = [[4 * i + j for j in range(4)] for i in range(ZN)]
    mine = lax.psum_scatter(mine, "dp", scatter_dimension=1, tiled=True, axis_index_groups=groups)
    mine = mine.astype(F32)
    return (mine[:RANK].T[None], mine[RANK:][None])


def solution(mesh):
    return jax.shard_map(
        shards,
        mesh=mesh,
        in_specs=(
            P(None, "dp", None),
            P(None, "dp"),
            P("pipe", None, None),
            P("pipe", None, None),
            P(),
            P(),
        ),
        out_specs=(P("pipe", "dp", None), P("pipe", None, "dp")),
        check_vma=False,
    )
```

time: 932 us -> 539 us (0.58)
  other arithmetic: 131 us -> 1.35 us
  matrix products: 122 us -> 0 us
  Pallas kernels: 0 us -> 122 us
  waiting for transfers between devices: 507 us -> 392 us
  starting transfers between devices: 73.5 us -> 0.16 us
  local copies, waits for them, and re-layouts: 64.9 us -> 7.43 us
  loops' own time: 15.8 us -> 0 us
    ppermute x22 -> x0, waiting for transfers between devices: 339 us -> none  [from_behind(): lax.ppermute(value, axis, [(source, source + steps) for source in range(f...]
    all_gather x0 -> x2, waiting for transfers between devices: none -> 183 us  [the longest x1 92.4 us: shards(): wu = lax.all_gather(up, 'pipe')]
    pallas_call x0 -> x1, Pallas kernels: none -> 122 us  [shards(): pl.pallas_call(kernel, out_shape=jax.ShapeDtypeStruct((LAYERS, 2 * RANK,...]
    dot_general x52 -> x0, matrix products: 122 us -> none  [the longest x22 45.6 us: contract_last(): lax.dot_general(left, right, (((1,), (1,)), ((), ())), preferred_element_...]
    ppermute x22 -> x0, starting transfers between devices: 73.4 us -> none  [from_behind(): lax.ppermute(value, axis, [(source, source + steps) for source in range(f...]
    convert_element_type x14 -> x1, other arithmetic: 47.3 us -> 1.16 us  [shards(): mine = mine.astype(F32)]
    reduce_scatter x2, waiting for transfers between devices: 168 us -> 209 us  [the longest x1 170 us: shards(): mine = lax.psum_scatter(part, 'pipe', scatter_dimension=0, tiled=True)[0]]
    dynamic_update_slice x22 -> x0, other arithmetic: 35 us -> none  [keep_slot(): lax.dynamic_update_index_in_dim(store, jnp.where(valid, value, former), p...]
  transfers between devices with their start and end apart: 24 -> 4, of which waited for: 24 -> 4; matrix products, arithmetic and copies ran while one was open for 6% -> 1% of each run, Pallas kernels for 0% -> 0%
where the time goes in v1:
time: 539 us; the launch traced here: 538 us
  waiting for transfers between devices  392 us (73%)
  Pallas kernels  122 us (23%)
  between operations  13.9 us (3%)
  local copies, waits for them, and re-layouts  7.43 us (1%)
    reduce_scatter x1, waiting for transfers between devices, shards(): mine = lax.psum_scatter(part, 'pipe', scatter_dimension=0, tiled=True)[0]  170 us
    pallas_call x1, Pallas kernels, shards(): pl.pallas_call(kernel, out_shape=jax.ShapeDtypeStruct((LAYERS, 2 * RANK,...  122 us
    all_gather x1, waiting for transfers between devices, shards(): wu = lax.all_gather(up, 'pipe')  92.4 us
    all_gather x1, waiting for transfers between devices, shards(): wd = lax.all_gather(down, 'pipe')  90.9 us
    reduce_scatter x1, waiting for transfers between devices, shards(): lax.psum_scatter(mine, 'dp', scatter_dimension=1, tiled=True, axis_index_...  39.6 us
  transfers between devices with their start and end apart: 4, of which 4 were waited for; matrix products, arithmetic and copies ran while one was open for 1% of the time, Pallas kernels for 0%

profile of v1, /device:TPU:0, one launch (start us, length us, event | category | flops | bytes accessed | tf_op | source)
XLA Modules:
  0.0 537.7 jit_solution(1422180808895176391)
XLA Ops:
  7.2 0.0 copy-start
  7.2 0.0 copy-start.1
  7.2 0.0 copy-start.3
  7.2 0.0 all-gather.3.cloned.1.call-start
  7.3 2.3 constant_dynamic-slice_fusion.1
  9.5 0.0 all-gather.3.cloned.1.call-update
  9.6 0.0 all-gather.5.cloned.1.call-start
  9.6 2.4 constant_dynamic-slice_fusion
  12.0 0.0 all-gather.5.cloned.1.call-update
  12.0 0.0 reduce-scatter.3.cloned.1.call-start
  12.1 0.0 copy-done.1
  12.1 0.6 reshape.12.vw_ref
  12.7 0.0 copy-done
  12.7 0.1 dynamic-slice_bitcast_fusion
  12.8 0.0 copy-done.3
  12.8 0.2 select_reduce_fusion
  13.0 0.2 dynamic_update_slice.3.tv_ref
  13.2 0.0 copy-start.2
  13.2 90.9 %all-gather.3.cloned.1.call-done.wd_hbm = bf16[8,2048,256]{2,1,0:T(8,128)(2,1)} async-done(((bf16[1,2048,256]{2,1,0:T(8,128)(2,1)}), bf16[8,2048,256]{2,1,0:T(8,128)(2,1)}) %all-gather.3.cloned.1.call-update) | async-done | bytes 8388624 | tf_op jit(solution)/shard_map/all_gather | solution.py:282
  104.1 92.4 %all-gather.5.cloned.1.call-done.wu_hbm = bf16[8,256,2048]{2,1,0:T(8,128)(2,1)} async-done(((bf16[1,256,2048]{2,1,0:T(8,128)(2,1)}), bf16[8,256,2048]{2,1,0:T(8,128)(2,1)}) %all-gather.5.cloned.1.call-update) | async-done | bytes 8388624 | tf_op jit(solution)/shard_map/all_gather | solution.py:283
  196.5 0.0 copy-done.2
  196.5 122.4 %relay.1 = bf16[8,512,2048]{2,1,0:T(8,128)(2,1)} custom-call(bf16[4,64,8192]{2,1,0:T(8,128)(2,1)} %x_hbm.1, bf16[8,2048,256]{2,1,0:T(8,128)(2,1)} %all-gather.3.cloned.1.call-done.wd_hbm, bf16[8,256,2048]{2,1,0:T(8,128)(2,1)} %all-gather.5.cloned.1.call-done.wu_hbm, f32[4,2048]{1,0:T(4,128)} %reshape.12.vw_ref, f32[8,128]{1,0:T(8,128)} %copy-done.2), custom_call_target="tpu_custom_call" | custom-call | tf_op jit(solution)/shard_map/relay/pallas_call | solution.py:290
  318.9 0.0 reduce-scatter.3.cloned.1.call-update
  319.0 0.0 reduce-scatter.5.cloned.1.call-start
  319.0 169.5 %reduce-scatter.3.cloned.1.call-done = bf16[1,512,2048]{2,1,0:T(8,128)(2,1)} async-done(((bf16[8,512,2048]{2,1,0:T(8,128)(2,1)}), bf16[1,512,2048]{2,1,0:T(8,128)(2,1)}) %reduce-scatter.3.cloned.1.call-update) | async-done | bytes 2097168 | tf_op jit(solution)/shard_map/reduce_scatter | solution.py:320
  488.5 0.0 reduce-scatter.5.cloned.1.call-update
  488.5 39.6 %reduce-scatter.5.cloned.1.call-done = bf16[512,512]{1,0:T(8,128)(2,1)} async-done(((bf16[512,2048]{1,0:T(8,128)(2,1)}), bf16[512,512]{1,0:T(8,128)(2,1)}) %reduce-scatter.5.cloned.1.call-update) | async-done | bytes 524304 | tf_op jit(solution)/shard_map/reduce_scatter | solution.py:322
  528.2 1.2 convert_element_type.3
  529.4 0.9 slice_bitcast_fusion
  530.2 1.0 copy.10
  (1 shorter events, 0.0 us)
Async XLA Ops:
  7.2 5.6 %copy-start = (s32[4,64]{1,0:T(4,128)S(1)}, s32[4,64]{1,0:T(4,128)}, u32[]{:S(2)}) copy-start(s32[4,64]{1,0:T(4,128)} %param.7) | copy-start | bytes 3076
  7.2 4.9 copy-start.1
  7.2 5.6 %copy-start.3 = (f32[512]{0:T(512)S(1)}, f32[512]{0:T(512)}, u32[]{:S(2)}) copy-start(f32[512]{0:T(512)} %param.11) | copy-start | bytes 6148
  7.2 96.9 %all-gather.3.cloned.1.call-start = ((), (), s32[]{:S(2)}) async-start(), calls=%async_computation.2 | async-start | bytes 9437184 | tf_op jit(solution)/shard_map/all_gather | solution.py:282
  9.6 186.9 %all-gather.5.cloned.1.call-start = ((), (), s32[]{:S(2)}) async-start(), calls=%async_computation.3 | async-start | bytes 9437184 | tf_op jit(solution)/shard_map/all_gather | solution.py:283
  12.0 476.5 %reduce-scatter.3.cloned.1.call-start = ((), (), s32[]{:S(2)}) async-start(), calls=%async_computation.4 | async-start | bytes 18874368 | tf_op jit(solution)/shard_map/reduce_scatter | solution.py:320
  13.2 183.3 %copy-start.2 = (f32[8,128]{1,0:T(8,128)}, f32[8,128]{1,0:T(8,128)S(1)}, u32[]{:S(2)}) copy-start(f32[8,128]{1,0:T(8,128)S(1)} %dynamic_update_slice.3.tv_ref) | copy-start | bytes 12292
  319.0 209.2 %reduce-scatter.5.cloned.1.call-start = ((), (), s32[]{:S(2)}) async-start(), calls=%async_computation.5 | async-start | bytes 2621440 | tf_op jit(solution)/shard_map/reduce_scatter | solution.py:322
Sparse Core Ops, SparseCore 0:
  9.7 94.3 all-gather.2
  105.7 90.6 all-gather.4
  319.1 169.4 reduce-scatter.2
  491.0 37.1 reduce-scatter.4

commit v2 on v1

--- a/solution.py
+++ b/solution.py
@@ -71,22 +71,46 @@
 
 
 def kernel(
-    x_hbm, wd_hbm, wu_hbm, vw_ref, tv_ref, out_hbm,
-    xs, wd, wu, snd, rcv, mine, gx, pre_s, act_s, scale_s, gbuf,
-    x_ssem, x_rsem, lsem, wsem, ssem, rsem, gsem,
+    x_hbm, wd_hbm, wu_hbm, vw_ref, tv_ref, out_ref,
+    xs, wd, wu, snd, rcv, mine, gx, pre_s, act_s, scale_s,
+    gbuf, cbuf, dsum, usum, d1, u1, d2s, u2s, d2, u2, d3s, u3s, res,
+    x_ssem, x_rsem, lsem, wsem, ssem, rsem,
+    y_ssem, y_rsem, n_ssem, n_rsem, c_ssem, c_rsem,
+    gc_ssem, gc_rsem, g1_ssem, g1_rsem, g2_ssem, g2_rsem, g3_ssem, g3_rsem,
 ):
     dp = lax.axis_index("dp")
     pipe = lax.axis_index("pipe")
     z = dp // 4
+    c = lax.rem(dp, 2)
+    xh = lax.rem(dp // 2, 2)
     rest = lax.rem(dp, 4)
     xl = pipe // 4
     y = lax.rem(pipe, 4)
+    x = xh * 2 + xl
     zs = [lax.rem(z + i, ZN) for i in range(1, ZN)]
     peers = [(zz * 4 + rest, pipe) for zz in zs]
-
-    for layer in range(LAYERS):
-        pltpu.make_async_copy(wd_hbm.at[layer], wd.at[layer], wsem.at[0, layer]).start()
-        pltpu.make_async_copy(wu_hbm.at[layer], wu.at[layer], wsem.at[1, layer]).start()
+    core_peer = (dp + 1 - 2 * c, pipe)
+
+    def x_dev(xx):
+        return (z * 4 + (xx // 2) * 2 + c, lax.rem(xx, 2) * 4 + y)
+
+    def y_dev(yy):
+        return (dp, xl * 4 + yy)
+
+    x_at = [lax.rem(x + i, 4) for i in range(1, 4)]
+    y_at = [lax.rem(y + i, 4) for i in range(1, 4)]
+
+    def remote(src, dst, send, recv, device):
+        return pltpu.make_async_remote_copy(
+            src_ref=src, dst_ref=dst, send_sem=send, recv_sem=recv,
+            device_id=device, device_id_type=MESH,
+        )
+
+    feats = pl.ds(pl.multiple_of(z * CH, CH), CH)
+    own_down = pltpu.make_async_copy(wd_hbm.at[0, feats, :], wd.at[pipe], wsem.at[0])
+    own_up = pltpu.make_async_copy(wu_hbm.at[0, :, feats], wu.at[pipe], wsem.at[1])
+    own_down.start()
+    own_up.start()
 
     def piece(zz):
         return x_hbm.at[y, pl.ds(pl.multiple_of(xl * OWN, OWN), OWN), pl.ds(pl.multiple_of(zz * CH, CH), CH)]
@@ -96,45 +120,100 @@
     own.start()
 
     barrier = pltpu.get_barrier_semaphore()
-    for peer in peers:
-        pl.semaphore_signal(barrier, inc=1, device_id=peer, device_id_type=MESH)
-    pl.semaphore_wait(barrier, ZN - 1)
+    greet = peers + [core_peer, x_dev(x_at[0]), x_dev(x_at[1]), x_dev(x_at[2])]
+    greet += [(dp, lax.rem(pipe + i, LAYERS)) for i in range(1, LAYERS)]
+    for device in greet:
+        pl.semaphore_signal(barrier, inc=1, device_id=device, device_id_type=MESH)
+    pl.semaphore_wait(barrier, len(greet))
+
+    HALF = CH // 2
+    QUART = CH // 4
+
+    def y_copy(which, i, layer):
+        at = pl.ds(pl.multiple_of(c * HALF, HALF), HALF)
+        far = pl.ds(pl.multiple_of(z * CH + c * HALF, HALF), HALF)
+        if which == 0:
+            src, dst = wd_hbm.at[0, far, :], wd.at[layer, at, :]
+        else:
+            src, dst = wu_hbm.at[0, :, far], wu.at[layer, :, at]
+        return remote(src, dst, y_ssem.at[which, i], y_rsem.at[which, layer], y_dev(y_at[i]))
+
+    def n_copy(which, layer, h):
+        at = pl.ds(pl.multiple_of(c * HALF + h * QUART, QUART), QUART)
+        ref = wd.at[layer, at, :] if which == 0 else wu.at[layer, :, at]
+        return remote(ref, ref, n_ssem.at[which, layer, h], n_rsem.at[which, layer, h], x_dev(x_at[2 * h]))
+
+    def c_copy(which, layer):
+        at = pl.ds(pl.multiple_of(c * HALF, HALF), HALF)
+        ref = wd.at[layer, at, :] if which == 0 else wu.at[layer, :, at]
+        return remote(ref, ref, c_ssem.at[which, layer], c_rsem.at[which, layer], core_peer)
 
     copies = []
     for i in range(ZN - 1):
-        copy = pltpu.make_async_remote_copy(
-            src_ref=piece(zs[i]), dst_ref=xs.at[0, own_rows],
-            send_sem=x_ssem.at[i], recv_sem=x_rsem.at[i],
-            device_id=peers[i], device_id_type=MESH,
-        )
+        copy = remote(piece(zs[i]), xs.at[0, own_rows], x_ssem.at[i], x_rsem.at[i], peers[i])
         copy.start()
         copies.append(copy)
-    own.wait()
-    for copy in copies:
-        copy.wait()
+    for which in (0, 1):
+        for i in (0, 2, 1):
+            y_copy(which, i, pipe).start()
+
+    def pass_on(which, layer):
+        in_column = layer // 4 == xl
+        is_own = layer == pipe
+
+        @pl.when(is_own)
+        def _():
+            (own_down if which == 0 else own_up).wait()
+
+        @pl.when(in_column & jnp.logical_not(is_own))
+        def _():
+            y_copy(which, 0, layer).wait_recv()
+
+        @pl.when(in_column)
+        def _():
+            n_copy(which, layer, 0).start()
+            n_copy(which, layer, 1).start()
+
+        @pl.when(jnp.logical_not(in_column))
+        def _():
+            n_copy(which, layer, 0).wait_recv()
+            n_copy(which, layer, 1).wait_recv()
+
+        @pl.when(jnp.logical_not(is_own))
+        def _():
+            c_copy(which, layer).start()
+
+    def wait_weights(which, layer):
+        @pl.when(layer != pipe)
+        def _():
+            c_copy(which, layer).wait_recv()
+
+    def sent_weights(which, layer):
+        @pl.when(layer // 4 == xl)
+        def _():
+            n_copy(which, layer, 0).wait_send()
+            n_copy(which, layer, 1).wait_send()
+
+        @pl.when(layer != pipe)
+        def _():
+            c_copy(which, layer).wait_send()
 
     def exchange(slot, rows):
-        copies = []
-        for i in range(ZN - 1):
-            copy = pltpu.make_async_remote_copy(
-                src_ref=snd.at[slot, pl.ds(0, rows)],
-                dst_ref=rcv.at[slot, i, pl.ds(0, rows)],
-                send_sem=ssem.at[slot, i], recv_sem=rsem.at[slot, i],
-                device_id=peers[i], device_id_type=MESH,
+        return [
+            remote(
+                snd.at[slot, pl.ds(0, rows)], rcv.at[slot, i, pl.ds(0, rows)],
+                ssem.at[slot, i], rsem.at[slot, i], peers[i],
             )
+            for i in range(ZN - 1)
+        ]
+
+    def begin(copies):
+        for copy in copies:
             copy.start()
-            copies.append(copy)
-        return copies
 
     def finish(copies):
         for copy in copies:
             copy.wait()
-
-    def wait_weights(which, layer):
-        if which == 0:
-            pltpu.make_async_copy(wd_hbm.at[layer], wd.at[layer], wsem.at[0, layer]).wait()
-        else:
-            pltpu.make_async_copy(wu_hbm.at[layer], wu.at[layer], wsem.at[1, layer]).wait()
 
     def cols(t):
         return slice(t * TILE, (t + 1) * TILE)
@@ -154,6 +233,9 @@
         return total
 
     snd[...] = jnp.zeros_like(snd)
+    own.wait()
+    finish(copies)
+    pass_on(0, 0)
     wait_weights(0, 0)
     product = jnp.zeros((TOK, RANK), F32)
     square = jnp.zeros((TOK, 128), F32)
@@ -163,12 +245,22 @@
         square += fold_lanes(wide_tile * wide_tile)
         product += dot(tile, wd[0, cols(t), :])
     own_row = send_product(0, product, square)
+    pass_on(1, 0)
+    pass_on(0, 1)
 
     def forward(layer, own_row):
         slot = lax.rem(layer, 2)
-        copies = exchange(slot, 16 + TOK)
-        wait_weights(1, layer)
-        finish(copies)
+        begin(exchange(slot, 16 + TOK))
+
+        @pl.when(layer < LAYERS - 1)
+        def _():
+            pass_on(1, layer + 1)
+
+        @pl.when(layer < LAYERS - 2)
+        def _():
+            pass_on(0, layer + 2)
+
+        finish(exchange(slot, 16 + TOK))
         total = mine[...]
         for i in range(ZN - 1):
             total = total + rcv[slot, i, 16 : 16 + TOK].astype(F32)
@@ -180,6 +272,7 @@
         pre_s[layer] = pre
         act_s[layer] = act
         after = jnp.minimum(layer + 1, LAYERS - 1)
+        wait_weights(1, layer)
 
         @pl.when(layer < LAYERS - 1)
         def _():
@@ -204,6 +297,12 @@
     value_row = row_sums(value_acc)
     target_row = tv_ref[0:1, :]
     snd[0, 0:16, 0:128] = pack_rows([own_row, value_row, target_row])
+    begin(exchange(0, 16))
+    for which in (0, 1):
+        for i in range(3):
+            y_copy(which, i, pipe).wait_send()
+        for layer in range(LAYERS):
+            sent_weights(which, layer)
     finish(exchange(0, 16))
     ssq = row_total(0, 0, own_row)
     raw = row_total(0, 3, value_row)
@@ -223,9 +322,110 @@
         product += dot_nt(tile, wu[LAYERS - 1, :, cols(t)])
     mine[...] = product
     snd[1, 16 : 16 + TOK] = product.astype(BF16)
-
-    def out_copy(layer, slot):
-        return pltpu.make_async_copy(gbuf.at[slot], out_hbm.at[layer], gsem.at[slot])
+    begin(exchange(1, 16 + TOK))
+
+    def core_copy(layer, half):
+        slot = lax.rem(layer, 2)
+        return remote(
+            gbuf.at[slot, 2 * half + 1 - c], cbuf.at[layer, half],
+            gc_ssem.at[slot, half], gc_rsem.at[layer, half], core_peer,
+        )
+
+    def first_copies(layer):
+        slot = lax.rem(layer, 2)
+        found = []
+        for i in range(3):
+            found.append(remote(
+                dsum.at[slot, x_at[i]], d1.at[layer, i],
+                g1_ssem.at[slot, 0, i], g1_rsem.at[layer, 0, i], x_dev(x_at[i]),
+            ))
+            found.append(remote(
+                usum.at[slot, y_at[i]], u1.at[layer, i],
+                g1_ssem.at[slot, 1, i], g1_rsem.at[layer, 1, i], y_dev(y_at[i]),
+            ))
+        return found
+
+    def second_copies(layer):
+        slot = lax.rem(layer, 2)
+        found = []
+        for i in range(3):
+            found.append(remote(
+                d2s.at[slot, y_at[i]], d2.at[layer, i],
+                g2_ssem.at[slot, 0, i], g2_rsem.at[layer, 0, i], y_dev(y_at[i]),
+            ))
+            found.append(remote(
+                u2s.at[slot, x_at[i]], u2.at[layer, i],
+                g2_ssem.at[slot, 1, i], g2_rsem.at[layer, 1, i], x_dev(x_at[i]),
+            ))
+        return found
+
+    def last_copies(layer):
+        return [
+            remote(src.at[layer], res.at[which, pipe], g3_ssem.at[layer, which], g3_rsem.at[which, pipe], (dp, layer))
+            for which, src in ((0, d3s), (1, u3s))
+        ]
+
+    def add_cores(layer):
+        slot = lax.rem(layer, 2)
+        for half in (0, 1):
+            core_copy(layer, half).wait()
+        for half in (0, 1):
+            for block in range(2):
+                for part in range(4):
+                    at = slice(block * 128 + part * 32, block * 128 + part * 32 + 32)
+                    dsum[slot, 2 * half + block, part] = (
+                        gbuf[slot, 2 * half + c, at].astype(F32) + cbuf[layer, half, at].astype(F32)
+                    ).astype(BF16)
+                    at = slice(RANK + at.start, RANK + at.stop)
+                    usum[slot, part, 2 * half + block] = (
+                        gbuf[slot, 2 * half + c, at].astype(F32) + cbuf[layer, half, at].astype(F32)
+                    ).astype(BF16)
+        begin(first_copies(layer))
+
+    def add_first(layer):
+        slot = lax.rem(layer, 2)
+        finish(first_copies(layer))
+        for part in range(4):
+            for total, at, got, to in ((dsum, x, d1, d2s), (usum, y, u1, u2s)):
+                value = total[slot, at, part].astype(F32)
+                for i in range(3):
+                    value = value + got[layer, i, part].astype(F32)
+                to[slot, part] = value.astype(BF16)
+        begin(second_copies(layer))
+
+    def add_second(layer):
+        slot = lax.rem(layer, 2)
+        finish(second_copies(layer))
+        done = []
+        for total, at, got in ((d2s, y, d2), (u2s, x, u2)):
+            value = total[slot, at].astype(F32)
+            for i in range(3):
+                value = value + got[layer, i].astype(F32)
+            done.append(value.astype(BF16))
+
+        @pl.when(layer == pipe)
+        def _():
+            res[0, pipe] = done[0]
+            res[1, pipe] = done[1]
+
+        @pl.when(layer != pipe)
+        def _():
+            d3s[layer] = done[0]
+            u3s[layer] = done[1]
+            begin(last_copies(layer))
+
+    def sums(step):
+        @pl.when((step >= 1) & (step < LAYERS + 1))
+        def _():
+            add_cores(LAYERS - step)
+
+        @pl.when((step >= 2) & (step < LAYERS + 2))
+        def _():
+            add_first(LAYERS + 1 - step)
+
+        @pl.when(step >= 3)
+        def _():
+            add_second(LAYERS + 2 - step)
 
     def backward(step, carry):
         layer = LAYERS - 1 - step
@@ -242,34 +442,57 @@
         grad_f = grad_pre.astype(F32)
         inner = jnp.sum(grad_f * pre, axis=1, keepdims=True) * (1.0 / FEAT)
         scaled = (grad_f * wide(scale, RANK)).astype(BF16)
-        on_x = wide(scale * scale * inner, TILE)
-        on_q = wide(scale, TILE)
-        below = jnp.maximum(layer - 1, 0)
-        product = jnp.zeros((TOK, RANK), F32)
+
+        @pl.when(layer > 0)
+        def _():
+            on_x = wide(scale * scale * inner, TILE)
+            on_q = wide(scale, TILE)
+            product = jnp.zeros((TOK, RANK), F32)
+            for t in range(CH // TILE):
+                q = dot_nt(grad_pre, wd[layer, cols(t), :])
+                tile = (
+                    gx[now, :, cols(t)].astype(F32) + on_q * q - on_x * xs[layer, :, cols(t)].astype(F32)
+                ).astype(BF16)
+                gx[1 - now, :, cols(t)] = tile
+                product += dot_nt(tile, wu[layer - 1, :, cols(t)])
+            mine[...] = product
+            snd[1 - slot, 16 : 16 + TOK] = product.astype(BF16)
+            begin(exchange(1 - slot, 16 + TOK))
+
+        act = act_s[layer]
+        turn = lax.rem(layer, 2)
         for t in range(CH // TILE):
-            q = dot_nt(grad_pre, wd[layer, cols(t), :])
-            tile = (
-                gx[now, :, cols(t)].astype(F32) + on_q * q - on_x * xs[layer, :, cols(t)].astype(F32)
-            ).astype(BF16)
-            gx[1 - now, :, cols(t)] = tile
-            product += dot_nt(tile, wu[below, :, cols(t)])
-        mine[...] = product
-        snd[1 - slot, 16 : 16 + TOK] = product.astype(BF16)
-
-        @pl.when(step >= 2)
-        def _():
-            out_copy(layer + 2, now).wait()
-
-        act = act_s[layer]
-        for t in range(CH // TILE):
-            gbuf[now, 0:RANK, cols(t)] = dot_tn(scaled, xs[layer, :, cols(t)]).astype(BF16)
-            gbuf[now, RANK : 2 * RANK, cols(t)] = dot_tn(act, gx[now, :, cols(t)]).astype(BF16)
-        out_copy(layer, now).start()
+            gbuf[turn, t, 0:RANK] = dot_tn(scaled, xs[layer, :, cols(t)]).astype(BF16)
+            gbuf[turn, t, RANK : 2 * RANK] = dot_tn(act, gx[now, :, cols(t)]).astype(BF16)
+        for half in (0, 1):
+            core_copy(layer, half).start()
+        sums(step)
         return carry
 
     lax.fori_loop(0, LAYERS, backward, 0)
-    out_copy(1, 0).wait()
-    out_copy(0, 1).wait()
+
+    def rest_of_sums(step, carry):
+        sums(step)
+        return carry
+
+    lax.fori_loop(LAYERS, LAYERS + 3, rest_of_sums, 0)
+
+    def finish_last(layer, carry):
+        @pl.when(layer != pipe)
+        def _():
+            for copy in last_copies(layer):
+                copy.wait_send()
+            for which in (0, 1):
+                remote(
+                    d3s.at[layer], res.at[which, layer],
+                    g3_ssem.at[layer, which], g3_rsem.at[which, layer], (dp, layer),
+                ).wait_recv()
+        return carry
+
+    lax.fori_loop(0, LAYERS, finish_last, 0)
+    for which in (0, 1):
+        for part in range(LAYERS):
+            out_ref[which, part * 32 : part * 32 + 32] = res[which, part]
 
 
 def shards(inputs, targets, adapter_down, adapter_up, value_weight, returns):
@@ -277,21 +500,18 @@
     pipe = lax.axis_index("pipe")
     z = dp // 4
     xl, y = pipe // 4, pipe % 4
-    down = lax.dynamic_slice_in_dim(adapter_down[0], z * CH, CH, 0)
-    up = lax.dynamic_slice_in_dim(adapter_up[0], z * CH, CH, 1)
-    wd = lax.all_gather(down, "pipe")
-    wu = lax.all_gather(up, "pipe")
     mine = lax.dynamic_slice(targets, (y, xl * OWN), (1, OWN))
     agents = jnp.arange(returns.shape[0], dtype=jnp.int32)
     values = jnp.sum(jnp.where(mine[0][:, None] == agents, returns, 0.0), axis=-1)
     tv = lax.dynamic_update_slice(jnp.zeros((8, 128), F32), values[None], (0, z * OWN))
     any_spec = pl.BlockSpec(memory_space=pl.ANY)
     vmem = pl.BlockSpec(memory_space=pltpu.VMEM)
+    dma = pltpu.SemaphoreType.DMA
     part = pl.pallas_call(
         kernel,
-        out_shape=jax.ShapeDtypeStruct((LAYERS, 2 * RANK, CH), BF16),
+        out_shape=jax.ShapeDtypeStruct((2, RANK, TILE), BF16),
         in_specs=[any_spec, any_spec, any_spec, vmem, vmem],
-        out_specs=any_spec,
+        out_specs=vmem,
         scratch_shapes=[
             pltpu.VMEM((LAYERS + 1, TOK, CH), BF16),
             pltpu.VMEM((LAYERS, CH, RANK), BF16),
@@ -303,25 +523,47 @@
             pltpu.VMEM((LAYERS, TOK, RANK), F32),
             pltpu.VMEM((LAYERS, TOK, RANK), BF16),
             pltpu.VMEM((LAYERS, TOK, 128), F32),
-            pltpu.VMEM((2, 2 * RANK, CH), BF16),
-            pltpu.SemaphoreType.DMA((ZN - 1,)),
-            pltpu.SemaphoreType.DMA((ZN - 1,)),
-            pltpu.SemaphoreType.DMA,
-            pltpu.SemaphoreType.DMA((2, LAYERS)),
-            pltpu.SemaphoreType.DMA((2, ZN - 1)),
-            pltpu.SemaphoreType.DMA((2, ZN - 1)),
-            pltpu.SemaphoreType.DMA((2,)),
+            pltpu.VMEM((2, 4, 2 * RANK, TILE), BF16),
+            pltpu.VMEM((LAYERS, 2, 2 * RANK, TILE), BF16),
+            pltpu.VMEM((2, 4, 4, 32, TILE), BF16),
+            pltpu.VMEM((2, 4, 4, 32, TILE), BF16),
+            pltpu.VMEM((LAYERS, 3, 4, 32, TILE), BF16),
+            pltpu.VMEM((LAYERS, 3, 4, 32, TILE), BF16),
+            pltpu.VMEM((2, 4, 32, TILE), BF16),
+            pltpu.VMEM((2, 4, 32, TILE), BF16),
+            pltpu.VMEM((LAYERS, 3, 32, TILE), BF16),
+            pltpu.VMEM((LAYERS, 3, 32, TILE), BF16),
+            pltpu.VMEM((LAYERS, 32, TILE), BF16),
+            pltpu.VMEM((LAYERS, 32, TILE), BF16),
+            pltpu.VMEM((2, LAYERS, 32, TILE), BF16),
+            dma((ZN - 1,)),
+            dma((ZN - 1,)),
+            dma,
+            dma((2,)),
+            dma((2, ZN - 1)),
+            dma((2, ZN - 1)),
+            dma((2, 3)),
+            dma((2, LAYERS)),
+            dma((2, LAYERS, 2)),
+            dma((2, LAYERS, 2)),
+            dma((2, LAYERS)),
+            dma((2, LAYERS)),
+            dma((2, 2)),
+            dma((LAYERS, 2)),
+            dma((2, 2, 3)),
+            dma((LAYERS, 2, 3)),
+            dma((2, 2, 3)),
+            dma((LAYERS, 2, 3)),
+            dma((LAYERS, 2)),
+            dma((2, LAYERS)),
         ],
         compiler_params=pltpu.CompilerParams(
-            collective_id=0, has_side_effects=True, vmem_limit_bytes=56 * 1024 * 1024
+            collective_id=0, has_side_effects=True, vmem_limit_bytes=60 * 1024 * 1024
         ),
         name="relay",
-    )(inputs, wd, wu, value_weight.reshape(ZN, CH), tv)
-    mine = lax.psum_scatter(part, "pipe", scatter_dimension=0, tiled=True)[0]
-    groups = [[4 * i + j for j in range(4)] for i in range(ZN)]
-    mine = lax.psum_scatter(mine, "dp", scatter_dimension=1, tiled=True, axis_index_groups=groups)
-    mine = mine.astype(F32)
-    return (mine[:RANK].T[None], mine[RANK:][None])
+    )(inputs, adapter_down, adapter_up, value_weight.reshape(ZN, CH), tv)
+    mine = part.astype(F32)
+    return (mine[0].T[None], mine[1][None])
 
 
 def solution(mesh):

time: 539 us -> 250 us (0.46)
  waiting for transfers between devices: 392 us -> 0 us
  Pallas kernels: 122 us -> 241 us
  between operations: 13.9 us -> 0.73 us
    reduce_scatter x2 -> x0, waiting for transfers between devices: 209 us -> none  [the longest x1 170 us: shards(): mine = lax.psum_scatter(part, 'pipe', scatter_dimension=0, tiled=True)[0]]
    all_gather x2 -> x0, waiting for transfers between devices: 183 us -> none  [the longest x1 92.4 us: shards(): wu = lax.all_gather(up, 'pipe')]
    pallas_call x1, Pallas kernels: 122 us -> 241 us  [shards(): pl.pallas_call(kernel, out_shape=jax.ShapeDtypeStruct((2, RANK, TILE), BF...]
  transfers between devices with their start and end apart: 4 -> 0, of which waited for: 4 -> 0; matrix products, arithmetic and copies ran while one was open for 1% -> 0% of each run, Pallas kernels for 0% -> 0%
where the time goes in v2:
time: 250 us; the launch traced here: 249 us
  Pallas kernels  241 us (96%)
  local copies, waits for them, and re-layouts  5.13 us (2%)
    pallas_call x1, Pallas kernels, shards(): pl.pallas_call(kernel, out_shape=jax.ShapeDtypeStruct((2, RANK, TILE), BF...  241 us

profile of v2, /device:TPU:0, one launch (start us, length us, event | category | flops | bytes accessed | tf_op | source)
XLA Modules:
  0.0 249.2 jit_solution(469227798257206260)
XLA Ops:
  0.6 0.0 copy-start
  0.7 0.6 copy-done
  1.3 0.1 dynamic-slice_bitcast_fusion
  1.4 0.9 select_reduce_fusion
  2.3 0.2 dynamic_update_slice.3.tv_ref
  2.5 0.0 copy-start.1
  2.5 1.4 reshape.8.vw_ref
  3.9 0.0 copy-done.1
  3.9 241.4 %relay.1 = bf16[2,256,512]{2,1,0:T(8,128)(2,1)} custom-call(bf16[4,64,8192]{2,1,0:T(8,128)(2,1)} %x_hbm.1, bf16[1,8192,256]{2,1,0:T(8,128)(2,1)} %wd_hbm.1, bf16[1,256,8192]{2,1,0:T(8,128)(2,1)} %wu_hbm.1, f32[4,2048]{1,0:T(4,128)} %reshape.8.vw_ref, f32[8,128]{1,0:T(8,128)} %copy-done.1), custom_call_target="tpu_custom_call" | custom-call | tf_op jit(solution)/shard_map/relay/pallas_call | solution.py:510
  245.2 1.8 slice.9
  247.0 1.2 convert_element_type.3
  248.2 1.0 copy.9
  (2 shorter events, 0.0 us)
Async XLA Ops:
  0.6 0.7 copy-start
  2.5 1.4 copy-start.1

commit v3 on v2

--- a/solution.py
+++ b/solution.py
@@ -71,11 +71,12 @@
 
 
 def kernel(
-    x_hbm, wd_hbm, wu_hbm, vw_ref, tv_ref, out_ref,
+    x_hbm, wd_hbm, wu_hbm, vw_hbm, ret_hbm, targets_ref, out_ref,
+    vw_s, ret_s,
     xs, wd, wu, snd, rcv, mine, gx, pre_s, act_s, scale_s,
     gbuf, cbuf, dsum, usum, d1, u1, d2s, u2s, d2, u2, d3s, u3s, res,
     x_ssem, x_rsem, lsem, wsem, ssem, rsem,
-    y_ssem, y_rsem, n_ssem, n_rsem, c_ssem, c_rsem,
+    y_ssem, y_rsem, r_ssem, r_rsem, vsem, n_ssem, n_rsem, c_ssem, c_rsem,
     gc_ssem, gc_rsem, g1_ssem, g1_rsem, g2_ssem, g2_rsem, g3_ssem, g3_rsem,
 ):
     dp = lax.axis_index("dp")
@@ -118,6 +119,13 @@
     own_rows = pl.ds(pl.multiple_of(z * OWN, OWN), OWN)
     own = pltpu.make_async_copy(piece(z), xs.at[0, own_rows], lsem)
     own.start()
+    small = pltpu.make_async_copy(vw_hbm.at[feats], vw_s.at[0], vsem.at[4])
+    small.start()
+    ret_copies = [
+        pltpu.make_async_copy(ret_hbm.at[pl.ds(128 * i, 128)], ret_s.at[i], vsem.at[i]) for i in range(4)
+    ]
+    for copy in ret_copies:
+        copy.start()
 
     barrier = pltpu.get_barrier_semaphore()
     greet = peers + [core_peer, x_dev(x_at[0]), x_dev(x_at[1]), x_dev(x_at[2])]
@@ -138,9 +146,16 @@
             src, dst = wu_hbm.at[0, :, far], wu.at[layer, :, at]
         return remote(src, dst, y_ssem.at[which, i], y_rsem.at[which, layer], y_dev(y_at[i]))
 
+    def quarter(which, layer, h):
+        at = pl.ds(pl.multiple_of(c * HALF + h * QUART, QUART), QUART)
+        return wd.at[layer, at, :] if which == 0 else wu.at[layer, :, at]
+
+    def r_copy(which, layer, h):
+        ref = quarter(which, layer, h)
+        return remote(ref, ref, r_ssem.at[which, h], r_rsem.at[which, h], y_dev(y_at[2 * h]))
+
     def n_copy(which, layer, h):
-        at = pl.ds(pl.multiple_of(c * HALF + h * QUART, QUART), QUART)
-        ref = wd.at[layer, at, :] if which == 0 else wu.at[layer, :, at]
+        ref = quarter(which, layer, h)
         return remote(ref, ref, n_ssem.at[which, layer, h], n_rsem.at[which, layer, h], x_dev(x_at[2 * h]))
 
     def c_copy(which, layer):
@@ -154,33 +169,34 @@
         copy.start()
         copies.append(copy)
     for which in (0, 1):
-        for i in (0, 2, 1):
+        for i in (0, 2):
             y_copy(which, i, pipe).start()
-
-    def pass_on(which, layer):
-        in_column = layer // 4 == xl
-        is_own = layer == pipe
-
-        @pl.when(is_own)
-        def _():
-            (own_down if which == 0 else own_up).wait()
-
-        @pl.when(in_column & jnp.logical_not(is_own))
-        def _():
+        (own_down if which == 0 else own_up).wait()
+        for h in (0, 1):
+            n_copy(which, pipe, h).start()
+
+    def column_layer(i):
+        return xl * 4 + y_at[i]
+
+    def spread(which):
+        for i, h in ((2, 0), (0, 1)):
+            layer = column_layer(i)
             y_copy(which, 0, layer).wait_recv()
-
-        @pl.when(in_column)
-        def _():
+            r_copy(which, layer, h).start()
+            c_copy(which, layer).start()
             n_copy(which, layer, 0).start()
             n_copy(which, layer, 1).start()
-
-        @pl.when(jnp.logical_not(in_column))
+        layer = column_layer(1)
+        for h in (0, 1):
+            r_copy(which, layer, h).wait_recv()
+            n_copy(which, layer, h).start()
+        c_copy(which, layer).start()
+
+    def pass_on(which, layer):
+        @pl.when(layer // 4 != xl)
         def _():
             n_copy(which, layer, 0).wait_recv()
             n_copy(which, layer, 1).wait_recv()
-
-        @pl.when(jnp.logical_not(is_own))
-        def _():
             c_copy(which, layer).start()
 
     def wait_weights(which, layer):
@@ -235,6 +251,22 @@
     snd[...] = jnp.zeros_like(snd)
     own.wait()
     finish(copies)
+    wanted = targets_ref[pl.ds(y, 1), :].astype(F32)
+    wanted = column(jnp.concatenate([wanted, jnp.zeros_like(wanted)], axis=1))
+    lane = lax.broadcasted_iota(jnp.int32, (TOK, 128), 1)
+    small.wait()
+    for copy in ret_copies:
+        copy.wait()
+    found = jnp.zeros((TOK, 128), F32)
+    for i in range(4):
+        agent = (lane + 128 * i).astype(F32)
+        found += jnp.where(wanted == agent, jnp.broadcast_to(ret_s[i : i + 1, :], (TOK, 128)), 0.0)
+    target_tile = pltpu.roll(
+        jnp.broadcast_to(row_sums(found), (8, 128)), lax.rem(z * OWN + 128 - xl * OWN, 128), axis=1
+    )
+    target_tile = jnp.where((lane[:8] >= z * OWN) & (lane[:8] < z * OWN + OWN), target_tile, 0.0)
+    target_row = target_tile[0:1]
+    spread(0)
     pass_on(0, 0)
     wait_weights(0, 0)
     product = jnp.zeros((TOK, RANK), F32)
@@ -245,12 +277,16 @@
         square += fold_lanes(wide_tile * wide_tile)
         product += dot(tile, wd[0, cols(t), :])
     own_row = send_product(0, product, square)
-    pass_on(1, 0)
-    pass_on(0, 1)
 
     def forward(layer, own_row):
         slot = lax.rem(layer, 2)
         begin(exchange(slot, 16 + TOK))
+
+        @pl.when(layer == 0)
+        def _():
+            pass_on(0, 1)
+            spread(1)
+            pass_on(1, 0)
 
         @pl.when(layer < LAYERS - 1)
         def _():
@@ -292,15 +328,16 @@
 
     value_acc = jnp.zeros((TOK, 128), F32)
     for t in range(CH // TILE):
-        weight = vw_ref[pl.ds(z, 1), cols(t)]
+        weight = vw_s[0:1, cols(t)]
         value_acc += fold_lanes(xs[LAYERS, :, cols(t)].astype(F32) * weight)
     value_row = row_sums(value_acc)
-    target_row = tv_ref[0:1, :]
     snd[0, 0:16, 0:128] = pack_rows([own_row, value_row, target_row])
     begin(exchange(0, 16))
     for which in (0, 1):
-        for i in range(3):
+        for i in (0, 2):
             y_copy(which, i, pipe).wait_send()
+        for h in (0, 1):
+            r_copy(which, pipe, h).wait_send()
         for layer in range(LAYERS):
             sent_weights(which, layer)
     finish(exchange(0, 16))
@@ -314,7 +351,7 @@
     on_x = column(-scale * scale * resid * value * (1.0 / FEAT))
     product = jnp.zeros((TOK, RANK), F32)
     for t in range(CH // TILE):
-        weight = vw_ref[pl.ds(z, 1), cols(t)]
+        weight = vw_s[0:1, cols(t)]
         tile = (
             wide(on_weight, TILE) * weight + wide(on_x, TILE) * xs[LAYERS, :, cols(t)].astype(F32)
         ).astype(BF16)
@@ -496,23 +533,17 @@
 
 
 def shards(inputs, targets, adapter_down, adapter_up, value_weight, returns):
-    dp = lax.axis_index("dp")
-    pipe = lax.axis_index("pipe")
-    z = dp // 4
-    xl, y = pipe // 4, pipe % 4
-    mine = lax.dynamic_slice(targets, (y, xl * OWN), (1, OWN))
-    agents = jnp.arange(returns.shape[0], dtype=jnp.int32)
-    values = jnp.sum(jnp.where(mine[0][:, None] == agents, returns, 0.0), axis=-1)
-    tv = lax.dynamic_update_slice(jnp.zeros((8, 128), F32), values[None], (0, z * OWN))
     any_spec = pl.BlockSpec(memory_space=pl.ANY)
     vmem = pl.BlockSpec(memory_space=pltpu.VMEM)
     dma = pltpu.SemaphoreType.DMA
     part = pl.pallas_call(
         kernel,
         out_shape=jax.ShapeDtypeStruct((2, RANK, TILE), BF16),
-        in_specs=[any_spec, any_spec, any_spec, vmem, vmem],
+        in_specs=[any_spec, any_spec, any_spec, any_spec, any_spec, vmem],
         out_specs=vmem,
         scratch_shapes=[
+            pltpu.VMEM((8, CH), F32),
+            pltpu.VMEM((8, 128), F32),
             pltpu.VMEM((LAYERS + 1, TOK, CH), BF16),
             pltpu.VMEM((LAYERS, CH, RANK), BF16),
             pltpu.VMEM((LAYERS, RANK, CH), BF16),
@@ -544,6 +575,9 @@
             dma((2, ZN - 1)),
             dma((2, 3)),
             dma((2, LAYERS)),
+            dma((2, 2)),
+            dma((2, 2)),
+            dma((5,)),
             dma((2, LAYERS, 2)),
             dma((2, LAYERS, 2)),
             dma((2, LAYERS)),
@@ -561,7 +595,7 @@
             collective_id=0, has_side_effects=True, vmem_limit_bytes=60 * 1024 * 1024
         ),
         name="relay",
-    )(inputs, adapter_down, adapter_up, value_weight.reshape(ZN, CH), tv)
+    )(inputs, adapter_down, adapter_up, value_weight, returns, targets)
     mine = part.astype(F32)
     return (mine[0].T[None], mine[1][None])
 

time: 250 us -> 205 us (0.82)
  Pallas kernels: 241 us -> 200 us
    pallas_call x1, Pallas kernels: 241 us -> 200 us  [shards(): pl.pallas_call(kernel, out_shape=jax.ShapeDtypeStruct((2, RANK, TILE), BF...]
where the time goes in v3:
time: 205 us
  Pallas kernels  200 us (98%)
  local copies, waits for them, and re-layouts  2.84 us (1%)
    pallas_call x1, Pallas kernels, shards(): pl.pallas_call(kernel, out_shape=jax.ShapeDtypeStruct((2, RANK, TILE), BF...  200 us

profile of v3, /device:TPU:0, one launch (start us, length us, event | category | flops | bytes accessed | tf_op | source)
XLA Modules:
  0.0 204.7 jit_solution(11800686531401333645)
XLA Ops:
  0.6 200.0 %relay.1 = bf16[2,256,512]{2,1,0:T(8,128)(2,1)} custom-call(bf16[4,64,8192]{2,1,0:T(8,128)(2,1)} %x_hbm.1, bf16[1,8192,256]{2,1,0:T(8,128)(2,1)} %wd_hbm.1, bf16[1,256,8192]{2,1,0:T(8,128)(2,1)} %wu_hbm.1, f32[8192]{0:T(1024)} %vw_hbm.1, f32[512]{0:T(512)} %ret_hbm.1, s32[4,64]{1,0:T(4,128)} %targets_ref.1), custom_call_target="tpu_custom_call" | custom-call | tf_op jit(solution)/shard_map/relay/pallas_call | solution.py:539
  200.6 1.8 slice.9
  202.5 1.2 convert_element_type.3
  203.7 1.0 copy.8
  (1 shorter events, 0.0 us)

commit v4 on v3

--- a/solution.py
+++ b/solution.py
@@ -71,7 +71,7 @@
 
 
 def kernel(
-    x_hbm, wd_hbm, wu_hbm, vw_hbm, ret_hbm, targets_ref, out_ref,
+    x_hbm, wd_hbm, wu_hbm, vw_hbm, ret_hbm, targets_ref, down_ref, up_ref,
     vw_s, ret_s,
     xs, wd, wu, snd, rcv, mine, gx, pre_s, act_s, scale_s,
     gbuf, cbuf, dsum, usum, d1, u1, d2s, u2s, d2, u2, d3s, u3s, res,
@@ -172,8 +172,15 @@
         for i in (0, 2):
             y_copy(which, i, pipe).start()
         (own_down if which == 0 else own_up).wait()
-        for h in (0, 1):
-            n_copy(which, pipe, h).start()
+        if which == 0:
+            for h in (0, 1):
+                n_copy(which, pipe, h).start()
+        else:
+
+            @pl.when(y < 2)
+            def _():
+                for h in (0, 1):
+                    n_copy(1, pipe, h).start()
 
     def column_layer(i):
         return xl * 4 + y_at[i]
@@ -184,13 +191,21 @@
             y_copy(which, 0, layer).wait_recv()
             r_copy(which, layer, h).start()
             c_copy(which, layer).start()
-            n_copy(which, layer, 0).start()
-            n_copy(which, layer, 1).start()
-        layer = column_layer(1)
-        for h in (0, 1):
-            r_copy(which, layer, h).wait_recv()
-            n_copy(which, layer, h).start()
-        c_copy(which, layer).start()
+        for j in range(4):
+            layer = xl * 4 + j
+
+            @pl.when(y_at[1] == j)
+            def _():
+                for h in (0, 1):
+                    r_copy(which, layer, h).wait_recv()
+                    n_copy(which, layer, h).start()
+                c_copy(which, layer).start()
+
+            later = (y == j) & (j >= 2) if which == 1 else False
+            @pl.when((y != j) & (y_at[1] != j) | later)
+            def _():
+                for h in (0, 1):
+                    n_copy(which, layer, h).start()
 
     def pass_on(which, layer):
         @pl.when(layer // 4 != xl)
@@ -226,6 +241,10 @@
     def begin(copies):
         for copy in copies:
             copy.start()
+
+    def begin_exchange(slot, rows):
+        first, far, last = exchange(slot, rows)
+        begin([far, first, last])
 
     def finish(copies):
         for copy in copies:
@@ -280,7 +299,7 @@
 
     def forward(layer, own_row):
         slot = lax.rem(layer, 2)
-        begin(exchange(slot, 16 + TOK))
+        begin_exchange(slot, 16 + TOK)
 
         @pl.when(layer == 0)
         def _():
@@ -332,7 +351,7 @@
         value_acc += fold_lanes(xs[LAYERS, :, cols(t)].astype(F32) * weight)
     value_row = row_sums(value_acc)
     snd[0, 0:16, 0:128] = pack_rows([own_row, value_row, target_row])
-    begin(exchange(0, 16))
+    begin_exchange(0, 16)
     for which in (0, 1):
         for i in (0, 2):
             y_copy(which, i, pipe).wait_send()
@@ -359,7 +378,7 @@
         product += dot_nt(tile, wu[LAYERS - 1, :, cols(t)])
     mine[...] = product
     snd[1, 16 : 16 + TOK] = product.astype(BF16)
-    begin(exchange(1, 16 + TOK))
+    begin_exchange(1, 16 + TOK)
 
     def core_copy(layer, half):
         slot = lax.rem(layer, 2)
@@ -369,7 +388,7 @@
         )
 
     def first_copies(layer):
-        slot = lax.rem(layer, 2)
+        slot = lax.rem(layer, 4)
         found = []
         for i in range(3):
             found.append(remote(
@@ -406,15 +425,16 @@
         slot = lax.rem(layer, 2)
         for half in (0, 1):
             core_copy(layer, half).wait()
+        deep = lax.rem(layer, 4)
         for half in (0, 1):
             for block in range(2):
                 for part in range(4):
                     at = slice(block * 128 + part * 32, block * 128 + part * 32 + 32)
-                    dsum[slot, 2 * half + block, part] = (
+                    dsum[deep, 2 * half + block, part] = (
                         gbuf[slot, 2 * half + c, at].astype(F32) + cbuf[layer, half, at].astype(F32)
                     ).astype(BF16)
                     at = slice(RANK + at.start, RANK + at.stop)
-                    usum[slot, part, 2 * half + block] = (
+                    usum[deep, part, 2 * half + block] = (
                         gbuf[slot, 2 * half + c, at].astype(F32) + cbuf[layer, half, at].astype(F32)
                     ).astype(BF16)
         begin(first_copies(layer))
@@ -424,7 +444,7 @@
         finish(first_copies(layer))
         for part in range(4):
             for total, at, got, to in ((dsum, x, d1, d2s), (usum, y, u1, u2s)):
-                value = total[slot, at, part].astype(F32)
+                value = total[lax.rem(layer, 4), at, part].astype(F32)
                 for i in range(3):
                     value = value + got[layer, i, part].astype(F32)
                 to[slot, part] = value.astype(BF16)
@@ -456,13 +476,13 @@
         def _():
             add_cores(LAYERS - step)
 
-        @pl.when((step >= 2) & (step < LAYERS + 2))
-        def _():
-            add_first(LAYERS + 1 - step)
-
-        @pl.when(step >= 3)
-        def _():
-            add_second(LAYERS + 2 - step)
+        @pl.when((step >= 3) & (step < LAYERS + 3))
+        def _():
+            add_first(LAYERS + 2 - step)
+
+        @pl.when(step >= 4)
+        def _():
+            add_second(LAYERS + 3 - step)
 
     def backward(step, carry):
         layer = LAYERS - 1 - step
@@ -494,7 +514,7 @@
                 product += dot_nt(tile, wu[layer - 1, :, cols(t)])
             mine[...] = product
             snd[1 - slot, 16 : 16 + TOK] = product.astype(BF16)
-            begin(exchange(1 - slot, 16 + TOK))
+            begin_exchange(1 - slot, 16 + TOK)
 
         act = act_s[layer]
         turn = lax.rem(layer, 2)
@@ -512,7 +532,7 @@
         sums(step)
         return carry
 
-    lax.fori_loop(LAYERS, LAYERS + 3, rest_of_sums, 0)
+    lax.fori_loop(LAYERS, LAYERS + 4, rest_of_sums, 0)
 
     def finish_last(layer, carry):
         @pl.when(layer != pipe)
@@ -527,20 +547,24 @@
         return carry
 
     lax.fori_loop(0, LAYERS, finish_last, 0)
-    for which in (0, 1):
-        for part in range(LAYERS):
-            out_ref[which, part * 32 : part * 32 + 32] = res[which, part]
+    down = jnp.concatenate([res[0, part].astype(F32) for part in range(LAYERS)], axis=0)
+    down_ref[...] = jnp.transpose(down).astype(BF16)
+    for part in range(LAYERS):
+        up_ref[part * 32 : part * 32 + 32] = res[1, part]
 
 
 def shards(inputs, targets, adapter_down, adapter_up, value_weight, returns):
     any_spec = pl.BlockSpec(memory_space=pl.ANY)
     vmem = pl.BlockSpec(memory_space=pltpu.VMEM)
     dma = pltpu.SemaphoreType.DMA
-    part = pl.pallas_call(
+    down, up = pl.pallas_call(
         kernel,
-        out_shape=jax.ShapeDtypeStruct((2, RANK, TILE), BF16),
+        out_shape=(
+            jax.ShapeDtypeStruct((TILE, RANK), BF16),
+            jax.ShapeDtypeStruct((RANK, TILE), BF16),
+        ),
         in_specs=[any_spec, any_spec, any_spec, any_spec, any_spec, vmem],
-        out_specs=vmem,
+        out_specs=(vmem, vmem),
         scratch_shapes=[
             pltpu.VMEM((8, CH), F32),
             pltpu.VMEM((8, 128), F32),
@@ -556,8 +580,8 @@
             pltpu.VMEM((LAYERS, TOK, 128), F32),
             pltpu.VMEM((2, 4, 2 * RANK, TILE), BF16),
             pltpu.VMEM((LAYERS, 2, 2 * RANK, TILE), BF16),
-            pltpu.VMEM((2, 4, 4, 32, TILE), BF16),
-            pltpu.VMEM((2, 4, 4, 32, TILE), BF16),
+            pltpu.VMEM((4, 4, 4, 32, TILE), BF16),
+            pltpu.VMEM((4, 4, 4, 32, TILE), BF16),
             pltpu.VMEM((LAYERS, 3, 4, 32, TILE), BF16),
             pltpu.VMEM((LAYERS, 3, 4, 32, TILE), BF16),
             pltpu.VMEM((2, 4, 32, TILE), BF16),
@@ -584,7 +608,7 @@
             dma((2, LAYERS)),
             dma((2, 2)),
             dma((LAYERS, 2)),
-            dma((2, 2, 3)),
+            dma((4, 2, 3)),
             dma((LAYERS, 2, 3)),
             dma((2, 2, 3)),
             dma((LAYERS, 2, 3)),
@@ -596,8 +620,7 @@
         ),
         name="relay",
     )(inputs, adapter_down, adapter_up, value_weight, returns, targets)
-    mine = part.astype(F32)
-    return (mine[0].T[None], mine[1][None])
+    return (down.astype(F32)[None], up.astype(F32)[None])
 
 
 def solution(mesh):

time: 205 us -> 206 us (level)
  local copies, waits for them, and re-layouts: 2.84 us -> 0 us
  other arithmetic: 1.16 us -> 3.58 us
    broadcast_in_dim x0 -> x2, other arithmetic: none -> 3.58 us  [shards(): return (down.astype(F32)[None], up.astype(F32)[None])]
    pallas_call x1, Pallas kernels: 200 us -> 202 us  [shards(): pl.pallas_call(kernel, out_shape=(jax.ShapeDtypeStruct((TILE, RANK), BF16...]
where the time goes in v4:
time: 206 us
  Pallas kernels  202 us (98%)
  other arithmetic  3.58 us (2%)
    pallas_call x1, Pallas kernels, shards(): pl.pallas_call(kernel, out_shape=(jax.ShapeDtypeStruct((TILE, RANK), BF16...  202 us

profile of v4, /device:TPU:0, one launch (start us, length us, event | category | flops | bytes accessed | tf_op | source)
XLA Modules:
  0.0 206.3 jit_solution(6747469088005862709)
XLA Ops:
  0.6 202.1 %relay.1 = (bf16[512,256]{1,0:T(8,128)(2,1)}, bf16[256,512]{1,0:T(8,128)(2,1)}) custom-call(bf16[4,64,8192]{2,1,0:T(8,128)(2,1)} %x_hbm.1, bf16[1,8192,256]{2,1,0:T(8,128)(2,1)} %wd_hbm.1, bf16[1,256,8192]{2,1,0:T(8,128)(2,1)} %wu_hbm.1, f32[8192]{0:T(1024)} %vw_hbm.1, f32[512]{0:T(512)} %ret_hbm.1, s32[4,64]{1,0:T(4,128)} %targets_ref.1), custom_call_target="tpu_custom_call" | custom-call | tf_op jit(solution)/shard_map/relay/pallas_call | solution.py:560
  202.7 1.8 bitcast_convert_fusion.1
  204.5 1.8 bitcast_convert_fusion

commit v5 on v4

--- a/solution.py
+++ b/solution.py
@@ -74,10 +74,10 @@
     x_hbm, wd_hbm, wu_hbm, vw_hbm, ret_hbm, targets_ref, down_ref, up_ref,
     vw_s, ret_s,
     xs, wd, wu, snd, rcv, mine, gx, pre_s, act_s, scale_s,
-    gbuf, cbuf, dsum, usum, d1, u1, d2s, u2s, d2, u2, d3s, u3s, res,
+    gbuf, cbuf, dsum, usum, m1, d1, u1, d2s, u2s, d2, u2, d3s, u3s, res,
     x_ssem, x_rsem, lsem, wsem, ssem, rsem,
     y_ssem, y_rsem, r_ssem, r_rsem, vsem, n_ssem, n_rsem, c_ssem, c_rsem,
-    gc_ssem, gc_rsem, g1_ssem, g1_rsem, g2_ssem, g2_rsem, g3_ssem, g3_rsem,
+    gc_ssem, gc_rsem, gm_ssem, gm_rsem, g1_ssem, g1_rsem, g2_ssem, g2_rsem, g3_ssem, g3_rsem,
 ):
     dp = lax.axis_index("dp")
     pipe = lax.axis_index("pipe")
@@ -168,7 +168,7 @@
         copy = remote(piece(zs[i]), xs.at[0, own_rows], x_ssem.at[i], x_rsem.at[i], peers[i])
         copy.start()
         copies.append(copy)
-    for which in (0, 1):
+    def start_own(which):
         for i in (0, 2):
             y_copy(which, i, pipe).start()
         (own_down if which == 0 else own_up).wait()
@@ -181,6 +181,8 @@
             def _():
                 for h in (0, 1):
                     n_copy(1, pipe, h).start()
+
+    start_own(0)
 
     def column_layer(i):
         return xl * 4 + y_at[i]
@@ -286,6 +288,7 @@
     target_tile = jnp.where((lane[:8] >= z * OWN) & (lane[:8] < z * OWN + OWN), target_tile, 0.0)
     target_row = target_tile[0:1]
     spread(0)
+    start_own(1)
     pass_on(0, 0)
     wait_weights(0, 0)
     product = jnp.zeros((TOK, RANK), F32)
@@ -387,17 +390,31 @@
             gc_ssem.at[slot, half], gc_rsem.at[layer, half], core_peer,
         )
 
-    def first_copies(layer):
-        slot = lax.rem(layer, 4)
+    def middle_copies(layer):
+        deep = lax.rem(layer, 4)
         found = []
-        for i in range(3):
+        for k, i in ((0, 0), (1, 2)):
             found.append(remote(
-                dsum.at[slot, x_at[i]], d1.at[layer, i],
-                g1_ssem.at[slot, 0, i], g1_rsem.at[layer, 0, i], x_dev(x_at[i]),
+                dsum.at[deep, x_at[1], pl.ds(2 * k, 2)], m1.at[0, layer, k],
+                gm_ssem.at[deep, 0, k], gm_rsem.at[layer, 0, k], x_dev(x_at[i]),
             ))
             found.append(remote(
-                usum.at[slot, y_at[i]], u1.at[layer, i],
-                g1_ssem.at[slot, 1, i], g1_rsem.at[layer, 1, i], y_dev(y_at[i]),
+                usum.at[deep, y_at[1], pl.ds(2 * k, 2)], m1.at[1, layer, k],
+                gm_ssem.at[deep, 1, k], gm_rsem.at[layer, 1, k], y_dev(y_at[i]),
+            ))
+        return found
+
+    def first_copies(layer):
+        deep = lax.rem(layer, 4)
+        found = []
+        for k, i in ((0, 0), (1, 2)):
+            found.append(remote(
+                dsum.at[deep, x_at[i]], d1.at[layer, k],
+                g1_ssem.at[deep, 0, k], g1_rsem.at[layer, 0, k], x_dev(x_at[i]),
+            ))
+            found.append(remote(
+                usum.at[deep, y_at[i]], u1.at[layer, k],
+                g1_ssem.at[deep, 1, k], g1_rsem.at[layer, 1, k], y_dev(y_at[i]),
             ))
         return found
 
@@ -437,6 +454,17 @@
                     usum[deep, part, 2 * half + block] = (
                         gbuf[slot, 2 * half + c, at].astype(F32) + cbuf[layer, half, at].astype(F32)
                     ).astype(BF16)
+        begin(middle_copies(layer))
+
+    def add_middle(layer):
+        deep = lax.rem(layer, 4)
+        finish(middle_copies(layer))
+        for k, i in ((0, 0), (1, 2)):
+            for part in range(2):
+                for which, total, at in ((0, dsum, x_at[i]), (1, usum, y_at[i])):
+                    total[deep, at, 2 * k + part] = (
+                        total[deep, at, 2 * k + part].astype(F32) + m1[which, layer, k, part].astype(F32)
+                    ).astype(BF16)
         begin(first_copies(layer))
 
     def add_first(layer):
@@ -445,7 +473,7 @@
         for part in range(4):
             for total, at, got, to in ((dsum, x, d1, d2s), (usum, y, u1, u2s)):
                 value = total[lax.rem(layer, 4), at, part].astype(F32)
-                for i in range(3):
+                for i in range(2):
                     value = value + got[layer, i, part].astype(F32)
                 to[slot, part] = value.astype(BF16)
         begin(second_copies(layer))
@@ -475,6 +503,10 @@
         @pl.when((step >= 1) & (step < LAYERS + 1))
         def _():
             add_cores(LAYERS - step)
+
+        @pl.when((step >= 2) & (step < LAYERS + 2))
+        def _():
+            add_middle(LAYERS + 1 - step)
 
         @pl.when((step >= 3) & (step < LAYERS + 3))
         def _():
@@ -582,8 +614,9 @@
             pltpu.VMEM((LAYERS, 2, 2 * RANK, TILE), BF16),
             pltpu.VMEM((4, 4, 4, 32, TILE), BF16),
             pltpu.VMEM((4, 4, 4, 32, TILE), BF16),
-            pltpu.VMEM((LAYERS, 3, 4, 32, TILE), BF16),
-            pltpu.VMEM((LAYERS, 3, 4, 32, TILE), BF16),
+            pltpu.VMEM((2, LAYERS, 2, 2, 32, TILE), BF16),
+            pltpu.VMEM((LAYERS, 2, 4, 32, TILE), BF16),
+            pltpu.VMEM((LAYERS, 2, 4, 32, TILE), BF16),
             pltpu.VMEM((2, 4, 32, TILE), BF16),
             pltpu.VMEM((2, 4, 32, TILE), BF16),
             pltpu.VMEM((LAYERS, 3, 32, TILE), BF16),
@@ -608,8 +641,10 @@
             dma((2, LAYERS)),
             dma((2, 2)),
             dma((LAYERS, 2)),
-            dma((4, 2, 3)),
-            dma((LAYERS, 2, 3)),
+            dma((4, 2, 2)),
+            dma((LAYERS, 2, 2)),
+            dma((4, 2, 2)),
+            dma((LAYERS, 2, 2)),
             dma((2, 2, 3)),
             dma((LAYERS, 2, 3)),
             dma((LAYERS, 2)),

time: 206 us -> 194 us (0.942)
  Pallas kernels: 202 us -> 189 us
    pallas_call x1, Pallas kernels: 202 us -> 189 us  [shards(): pl.pallas_call(kernel, out_shape=(jax.ShapeDtypeStruct((TILE, RANK), BF16...]
where the time goes in v5:
time: 194 us
  Pallas kernels  189 us (97%)
  other arithmetic  3.58 us (2%)
    pallas_call x1, Pallas kernels, shards(): pl.pallas_call(kernel, out_shape=(jax.ShapeDtypeStruct((TILE, RANK), BF16...  189 us

profile of v5, /device:TPU:0, one launch (start us, length us, event | category | flops | bytes accessed | tf_op | source)
XLA Modules:
  0.0 193.6 jit_solution(11355689483699600970)
XLA Ops:
  0.6 189.3 %relay.1 = (bf16[512,256]{1,0:T(8,128)(2,1)}, bf16[256,512]{1,0:T(8,128)(2,1)}) custom-call(bf16[4,64,8192]{2,1,0:T(8,128)(2,1)} %x_hbm.1, bf16[1,8192,256]{2,1,0:T(8,128)(2,1)} %wd_hbm.1, bf16[1,256,8192]{2,1,0:T(8,128)(2,1)} %wu_hbm.1, f32[8192]{0:T(1024)} %vw_hbm.1, f32[512]{0:T(512)} %ret_hbm.1, s32[4,64]{1,0:T(4,128)} %targets_ref.1), custom_call_target="tpu_custom_call" | custom-call | tf_op jit(solution)/shard_map/relay/pallas_call | solution.py:592
  190.0 1.8 bitcast_convert_fusion.1
  191.8 1.8 bitcast_convert_fusion

commit v6 on v5

--- a/solution.py
+++ b/solution.py
@@ -270,8 +270,6 @@
         return total
 
     snd[...] = jnp.zeros_like(snd)
-    own.wait()
-    finish(copies)
     wanted = targets_ref[pl.ds(y, 1), :].astype(F32)
     wanted = column(jnp.concatenate([wanted, jnp.zeros_like(wanted)], axis=1))
     lane = lax.broadcasted_iota(jnp.int32, (TOK, 128), 1)
@@ -288,6 +286,8 @@
     target_tile = jnp.where((lane[:8] >= z * OWN) & (lane[:8] < z * OWN + OWN), target_tile, 0.0)
     target_row = target_tile[0:1]
     spread(0)
+    own.wait()
+    finish(copies)
     start_own(1)
     pass_on(0, 0)
     wait_weights(0, 0)

time: 194 us -> 194 us (level)
  no operation moved by 1% of the time
where the time goes in v6:
time: 194 us
  Pallas kernels  189 us (97%)
  other arithmetic  3.58 us (2%)
    pallas_call x1, Pallas kernels, shards(): pl.pallas_call(kernel, out_shape=(jax.ShapeDtypeStruct((TILE, RANK), BF16...  189 us

profile of v6, /device:TPU:0, one launch (start us, length us, event | category | flops | bytes accessed | tf_op | source)
XLA Modules:
  0.0 193.6 jit_solution(10439977520954355543)
XLA Ops:
  0.6 189.4 %relay.1 = (bf16[512,256]{1,0:T(8,128)(2,1)}, bf16[256,512]{1,0:T(8,128)(2,1)}) custom-call(bf16[4,64,8192]{2,1,0:T(8,128)(2,1)} %x_hbm.1, bf16[1,8192,256]{2,1,0:T(8,128)(2,1)} %wd_hbm.1, bf16[1,256,8192]{2,1,0:T(8,128)(2,1)} %wu_hbm.1, f32[8192]{0:T(1024)} %vw_hbm.1, f32[512]{0:T(512)} %ret_hbm.1, s32[4,64]{1,0:T(4,128)} %targets_ref.1), custom_call_target="tpu_custom_call" | custom-call | tf_op jit(solution)/shard_map/relay/pallas_call | solution.py:592
  190.0 1.8 bitcast_convert_fusion.1
  191.8 1.8 bitcast_convert_fusion

commit v7 on v5

--- a/solution.py
+++ b/solution.py
@@ -306,17 +306,13 @@
 
         @pl.when(layer == 0)
         def _():
-            pass_on(0, 1)
             spread(1)
-            pass_on(1, 0)
+
+        pass_on(1, layer)
 
         @pl.when(layer < LAYERS - 1)
         def _():
-            pass_on(1, layer + 1)
-
-        @pl.when(layer < LAYERS - 2)
-        def _():
-            pass_on(0, layer + 2)
+            pass_on(0, layer + 1)
 
         finish(exchange(slot, 16 + TOK))
         total = mine[...]

time: 194 us -> 191 us (0.985)
  Pallas kernels: 189 us -> 186 us
    pallas_call x1, Pallas kernels: 189 us -> 186 us  [shards(): pl.pallas_call(kernel, out_shape=(jax.ShapeDtypeStruct((TILE, RANK), BF16...]
where the time goes in v7:
time: 191 us; the launch traced here: 190 us
  Pallas kernels  186 us (97%)
  other arithmetic  3.58 us (2%)
    pallas_call x1, Pallas kernels, shards(): pl.pallas_call(kernel, out_shape=(jax.ShapeDtypeStruct((TILE, RANK), BF16...  186 us

profile of v7, /device:TPU:0, one launch (start us, length us, event | category | flops | bytes accessed | tf_op | source)
XLA Modules:
  0.0 190.4 jit_solution(11694334592425248477)
XLA Ops:
  0.6 186.2 %relay.1 = (bf16[512,256]{1,0:T(8,128)(2,1)}, bf16[256,512]{1,0:T(8,128)(2,1)}) custom-call(bf16[4,64,8192]{2,1,0:T(8,128)(2,1)} %x_hbm.1, bf16[1,8192,256]{2,1,0:T(8,128)(2,1)} %wd_hbm.1, bf16[1,256,8192]{2,1,0:T(8,128)(2,1)} %wu_hbm.1, f32[8192]{0:T(1024)} %vw_hbm.1, f32[512]{0:T(512)} %ret_hbm.1, s32[4,64]{1,0:T(4,128)} %targets_ref.1), custom_call_target="tpu_custom_call" | custom-call | tf_op jit(solution)/shard_map/relay/pallas_call | solution.py:588
  186.8 1.8 bitcast_convert_fusion.1
  188.6 1.8 bitcast_convert_fusion
